TPU v7x, 32 devices: a whole 2x2x4 slice. The times are simulated.
32 devices in a mesh: cube: 4 (over y, x), blk: 8 (over z, core).
Axes of the slice: x: 2, y: 2, z: 4, core: 2. Of those that a mesh axis runs over, the one named last changes fastest.
Arguments:
- updates: float32 [4, 8, 8, 128, 128], P('cube', 'blk'), may hold values from -6 to 6
- pivot_panel: float32 [2048, 256], P(('cube', 'blk')), may hold values from -1.5 to 1.5
- map_low: int32 [4, 8, 8], P('cube', 'blk'), may hold values from 0 to 7
- map_own: int32 [4, 8, 8], P('cube', 'blk'), may hold values from 0 to 7
- map_out: int32 [4, 8, 8], P('cube', 'blk'), may hold values from 0 to 7
Outputs:
- schur: float32 [4, 8, 64, 2048], P(None, 'blk', None, 'cube')
All inputs are finite; a program needn't handle non-finite values.
Results may differ from a plain program's by a relative error of at most 0.000058.
Values sent between devices are 32-bit elements; how exact they have to be, the bound alone decides.
No kernel may reach another device: no remote copies, remote signals or barrier semaphores. Data moves between devices by JAX's collectives and lax.ppermute only.
A program may use at most 64 MiB of HBM per device.

v0:
```python
import jax
import jax.numpy as jnp
from jax import lax
from jax.sharding import PartitionSpec as P

exact_mode = lax.Precision.HIGHEST


def swapped(shard, axis, bit):
    return lax.ppermute(shard, axis, [(i, i ^ 1 << bit) for i in range(lax.axis_size(axis))])


def one_hot(targets, classes):
    return (targets[:, None] == jnp.arange(classes, dtype=jnp.int32)).astype(jnp.float32)


def scatter_slots(targets, classes, blocks):
    return jnp.dot(
        one_hot(targets, classes).T,
        blocks,
        precision=exact_mode,
        preferred_element_type=jnp.float32,
    )


def local(updates, pivot_panel, map_low, map_own, map_out):
    bit_count = lax.axis_size("cube").bit_length() - 1
    block_count = updates.shape[2]
    tile_size = updates.shape[3]
    part_rows = pivot_panel.shape[0]
    row_count = lax.axis_size("cube") * part_rows
    col_count = lax.axis_size("blk") * part_rows
    tile_count = row_count // tile_size * (col_count // tile_size)
    blocks = updates.reshape(block_count, tile_size * tile_size)
    low_targets = map_low.reshape(block_count)
    out_targets = map_out.reshape(block_count)
    outgoing = scatter_slots(low_targets, block_count, blocks)
    merged = blocks + swapped(outgoing, "cube", bit_count - 2)
    assembled = scatter_slots(map_own.reshape(block_count), tile_count, merged)
    peer_blocks, peer_map = swapped((merged, out_targets), "cube", bit_count - 1)
    assembled = assembled + scatter_slots(peer_map, tile_count, peer_blocks)
    row_panel = lax.all_gather(pivot_panel, "cube", axis=0, tiled=True)
    contribution = lax.dot_general(
        row_panel,
        lax.all_gather(pivot_panel, "blk", axis=0, tiled=True),
        (((1,), (1,)), ((), ())),
        precision=exact_mode,
        preferred_element_type=jnp.float32,
    )
    tile_grid = assembled.reshape(
        row_count // tile_size, col_count // tile_size, tile_size, tile_size
    )
    front_block = tile_grid.transpose(0, 2, 1, 3).reshape(row_count, col_count)
    schur_block = front_block - contribution
    return schur_block.reshape(lax.axis_size("cube"), 1, part_rows, col_count)


def solution(mesh):
    placed = (
        P("cube", "blk", None, None, None),
        P(("cube", "blk"), None),
        P("cube", "blk", None),
        P("cube", "blk", None),
        P("cube", "blk", None),
    )
    return jax.shard_map(
        local, mesh=mesh, in_specs=placed, out_specs=P(None, "blk", None, "cube"), check_vma=False
    )
```

profile of v0, /device:TPU:0, one launch (start us, length us, event | category | flops | bytes accessed | tf_op | source)
XLA Modules:
  0.0 54.8 jit_solution(449275329120546004)
XLA Ops:
  0.0 0.0 copy-start.2
  0.0 0.7 %copy-done.2 = s32[1,1,8]{2,1,0:T(1,128)S(1)} copy-done((s32[1,1,8]{2,1,0:T(1,128)S(1)}, s32[1,1,8]{2,1,0:T(1,128)}, u32[]{:S(2)}) %copy-start.2) | copy-done | bytes 56
  0.7 0.0 copy-start
  0.7 1.8 %fusion.1 = f32[8,16384]{1,0:T(8,128)S(1)} fusion(f32[1,8,128,128]{3,2,1,0:T(8,128)} %bitcast.27, s32[8]{0:T(128)S(1)} %bitcast.30), kind=kOutput, calls=%fused_computation.4 | convolution fusion | flops 12582976 | bytes 1048608 | tf_op jit(solution)/shard_map/dot_general | solution.py:18
  2.5 0.0 copy-start.1
  2.5 3.0 %collective-permute-start = (f32[8,16384]{1,0:T(8,128)S(1)}, f32[8,16384]{1,0:T(8,128)S(1)}, u32[]{:S(2)}, u32[]{:S(2)}) collective-permute-start(f32[8,16384]{1,0:T(8,128)S(1)} %fusion.1), channel_id=1, source_target_pairs={{0,8},{8,0},{16,24},{24,16},{1,9},{9,1},{17,25},{25,17},{2,10},{10... | collective-permute-start | bytes 1572872 | tf_op jit(solution)/shard_map/ppermute | solution.py:10
  5.5 11.9 %collective-permute-done = f32[8,16384]{1,0:T(8,128)S(1)} collective-permute-done((f32[8,16384]{1,0:T(8,128)S(1)}, f32[8,16384]{1,0:T(8,128)S(1)}, u32[]{:S(2)}, u32[]{:S(2)}) %collective-permute-start) | collective-permute-done | bytes 524320 | tf_op jit(solution)/shard_map/ppermute | solution.py:10
  17.4 0.0 copy-done
  17.4 0.3 bitcast_add_fusion
  17.8 0.0 copy-start.4
  17.8 1.8 %collective-permute-start.2 = (f32[8,16384]{1,0:T(8,128)S(1)}, f32[8,16384]{1,0:T(8,128)S(1)}, u32[]{:S(2)}, u32[]{:S(2)}) collective-permute-start(f32[8,16384]{1,0:T(8,128)S(1)} %bitcast_add_fusion), channel_id=1, source_target_pairs={{0,16},{8,24},{16,0},{24,8},{1,17},{9,25},{17,1},{25,9},{2,18},{10... | collective-permute-start | bytes 1572872 | tf_op jit(solution)/shard_map/ppermute | solution.py:10
  19.6 0.0 copy-done.4
  19.6 0.6 %collective-permute-start.1 = (s32[8]{0:T(128)S(1)}, s32[8]{0:T(128)S(1)}, u32[]{:S(2)}, u32[]{:S(2)}) collective-permute-start(s32[8]{0:T(128)S(1)} %bitcast.32), channel_id=1, source_target_pairs={{0,16},{8,24},{16,0},{24,8},{1,17},{9,25},{17,1},{25,9},{2,18},{10... | collective-permute-start | bytes 104 | tf_op jit(solution)/shard_map/ppermute | solution.py:10
  20.2 0.0 copy-done.1
  20.2 15.3 %all_gather.6 = f32[256,256]{1,0:T(8,128)S(1)} all-gather(f32[64,256]{1,0:T(8,128)S(1)} %copy-done.1), channel_id=1, replica_groups=mesh['cube'=4,'blk'=8] {'cube'}, dimensions={0}, use_global_device_ids=true | all-gather | bytes 327680 | tf_op jit(solution)/shard_map/all_gather | solution.py:42
  35.5 15.8 %all_gather.7 = f32[512,256]{1,0:T(8,128)S(1)} all-gather(f32[64,256]{1,0:T(8,128)S(1)} %copy-done.1), channel_id=1, replica_groups=mesh['cube'=4,'blk'=8] {'blk'}, dimensions={0}, use_global_device_ids=true | all-gather | bytes 589824 | tf_op jit(solution)/shard_map/all_gather | solution.py:45
  51.3 0.0 collective-permute-done.1
  51.3 0.0 collective-permute-done.2
  51.3 0.5 fusion.4
  51.8 0.0 copy-start.3
  51.8 0.6 %copy-done.3 = s32[1,1,8]{2,1,0:T(1,128)S(1)} copy-done((s32[1,1,8]{2,1,0:T(1,128)S(1)}, s32[1,1,8]{2,1,0:T(1,128)}, u32[]{:S(2)}) %copy-start.3) | copy-done | bytes 56
  52.4 0.5 fusion
  52.9 0.1 copy.9
  53.0 0.3 copy.6
  53.4 1.4 %convolution_subtract_fusion = f32[256,512]{1,0:T(8,128)} fusion(f32[256,256]{1,0:T(8,128)S(1)} %all_gather.6, f32[512,256]{1,0:T(8,128)S(1)} %all_gather.7, f32[32,8,4,128]{3,2,1,0:T(4,128)S(1)} %bitcast.26), kind=kOutput, calls=%fused_computation.2 | convolution fusion | flops 402784256 | bytes 1835008 | tf_op jit(solution)/shard_map/dot_general | solution.py:43
Async XLA Ops:
  0.0 0.7 %copy-start.2 = (s32[1,1,8]{2,1,0:T(1,128)S(1)}, s32[1,1,8]{2,1,0:T(1,128)}, u32[]{:S(2)}) copy-start(s32[1,1,8]{2,1,0:T(1,128)} %param.7) | copy-start | bytes 100
  0.7 16.8 %copy-start = (f32[1,1,8,128,128]{4,3,2,1,0:T(8,128)S(1)}, f32[1,1,8,128,128]{4,3,2,1,0:T(8,128)}, u32[]{:S(2)}) copy-start(f32[1,1,8,128,128]{4,3,2,1,0:T(8,128)} %param.5) | copy-start | bytes 1572868
  2.5 17.7 %copy-start.1 = (f32[64,256]{1,0:T(8,128)S(1)}, f32[64,256]{1,0:T(8,128)}, u32[]{:S(2)}) copy-start(f32[64,256]{1,0:T(8,128)} %param.6) | copy-start | bytes 196612
  2.5 14.9 %collective-permute-start = (f32[8,16384]{1,0:T(8,128)S(1)}, f32[8,16384]{1,0:T(8,128)S(1)}, u32[]{:S(2)}, u32[]{:S(2)}) collective-permute-start(f32[8,16384]{1,0:T(8,128)S(1)} %fusion.1), channel_id=1, source_target_pairs={{0,8},{8,0},{16,24},{24,16},{1,9},{9,1},{17,25},{25,17},{2,10},{10... | collective-permute-start | bytes 1572872 | tf_op jit(solution)/shard_map/ppermute | solution.py:10
  17.8 1.8 %copy-start.4 = (s32[1,1,8]{2,1,0:T(1,128)S(1)}, s32[1,1,8]{2,1,0:T(1,128)}, u32[]{:S(2)}) copy-start(s32[1,1,8]{2,1,0:T(1,128)} %param.9) | copy-start | bytes 100
  17.8 33.5 %collective-permute-start.2 = (f32[8,16384]{1,0:T(8,128)S(1)}, f32[8,16384]{1,0:T(8,128)S(1)}, u32[]{:S(2)}, u32[]{:S(2)}) collective-permute-start(f32[8,16384]{1,0:T(8,128)S(1)} %bitcast_add_fusion), channel_id=1, source_target_pairs={{0,16},{8,24},{16,0},{24,8},{1,17},{9,25},{17,1},{25,9},{2,18},{10... | collective-permute-start | bytes 1572872 | tf_op jit(solution)/shard_map/ppermute | solution.py:10
  19.6 31.7 %collective-permute-start.1 = (s32[8]{0:T(128)S(1)}, s32[8]{0:T(128)S(1)}, u32[]{:S(2)}, u32[]{:S(2)}) collective-permute-start(s32[8]{0:T(128)S(1)} %bitcast.32), channel_id=1, source_target_pairs={{0,16},{8,24},{16,0},{24,8},{1,17},{9,25},{17,1},{25,9},{2,18},{10... | collective-permute-start | bytes 104 | tf_op jit(solution)/shard_map/ppermute | solution.py:10
  51.8 0.7 %copy-start.3 = (s32[1,1,8]{2,1,0:T(1,128)S(1)}, s32[1,1,8]{2,1,0:T(1,128)}, u32[]{:S(2)}) copy-start(s32[1,1,8]{2,1,0:T(1,128)} %param.8) | copy-start | bytes 100
where the time goes:
time: 55 us; the launch traced here: 54.8 us
  blocking collectives  31.1 us (57%)
  waiting for transfers between devices  11.9 us (22%)
  starting transfers between devices  5.42 us (10%)
  matrix products  4.21 us (8%)
  local copies, waits for them, and re-layouts  1.77 us (3%)
    all_gather x1, blocking collectives, local(): lax.all_gather(pivot_panel, 'blk', axis=0, tiled=True)  15.8 us
    all_gather x1, blocking collectives, local(): row_panel = lax.all_gather(pivot_panel, 'cube', axis=0, tiled=True)  15.3 us
    ppermute x3, waiting for transfers between devices, swapped(): lax.ppermute(shard, axis, [(i, i ^ 1 << bit) for i in range(lax.axis_size...  11.9 us
    ppermute x3, starting transfers between devices, swapped(): lax.ppermute(shard, axis, [(i, i ^ 1 << bit) for i in range(lax.axis_size...  5.42 us
    dot_general x3, matrix products, scatter_slots(): jnp.dot(one_hot(targets, classes).T, blocks, precision=exact_mode, prefer...  2.79 us
    dot_general x1, matrix products, local(): lax.dot_general(row_panel, lax.all_gather(pivot_panel, 'blk', axis=0, til...  1.43 us
    unnamed x11, local copies, waits for them, and re-layouts  1.42 us
  transfers between devices with their start and end apart: 3, of which 1 were waited for; matrix products, arithmetic and copies ran while one was open for 0% of the time, Pallas kernels for 0%

commit v1 on v0

v1 whole, which is shorter than its diff:
```python
import functools

import jax
import jax.numpy as jnp
from jax import lax
from jax.experimental import pallas as pl
from jax.experimental.pallas import tpu as pltpu
from jax.sharding import PartitionSpec as P

AXES = ("cube", "blk")
VMEM = pl.BlockSpec(memory_space=pltpu.VMEM)
SMEM = pl.BlockSpec(memory_space=pltpu.SMEM)


class Plan:
    def __init__(self, tile_count, block_count):
        self.cubes, self.blks = lax.axis_size("cube"), lax.axis_size("blk")
        bit_count = self.cubes.bit_length() - 1
        self.low, self.up = 1 << (bit_count - 2), 1 << (bit_count - 1)
        self.balanced = tile_count <= block_count

    def turned(self, b):
        return self.balanced and b % 2 == 1

    def offset(self, b, stage):
        return self.up if self.turned(b) == (stage == 0) else self.low

    def swap(self, shard, stage):
        pairs = [
            (c * self.blks + b, (c ^ self.offset(b, stage)) * self.blks + b)
            for c in range(self.cubes)
            for b in range(self.blks)
        ]
        return lax.ppermute(shard, AXES, pairs)

    def is_turned(self):
        return lax.rem(lax.axis_index("blk"), 2) == 1 if self.balanced else jnp.bool_(False)


def flipped(shard, axis, offset):
    return lax.ppermute(shard, axis, [(i, i ^ offset) for i in range(lax.axis_size(axis))])


def send_kernel(plan, block_count, low, out, low_met, own_other, out_far, mine, met, sent):
    turned = plan.is_turned()
    sent[...] = jnp.zeros_like(sent)
    for u in range(block_count):
        if plan.balanced:
            slot = jnp.where(turned, own_other[0, 0, low[0, 0, u]], out[0, 0, u])
        else:
            slot = u
        sent[slot] += mine[0, 0, u]
    for u in range(block_count):
        slot = low_met[0, 0, u]
        if plan.balanced:
            slot = jnp.where(turned, out_far[0, 0, slot], out[0, 0, slot])
        sent[slot] += met[0, 0, u]


def part_kernel(plan, block_count, row_offsets, col_offsets, own, low_met, out_met, *refs):
    rows, cols = len(row_offsets), len(col_offsets)
    mine, met = refs[:2]
    row_refs, col_refs = refs[2 : 2 + rows], refs[2 + rows : 2 + rows + cols]
    part, tiles, left, right = refs[2 + rows + cols :]
    part_rows = row_refs[0].shape[0]
    turned = plan.is_turned()
    tiles[...] = jnp.zeros_like(tiles)
    for u in range(block_count):
        tiles[own[0, 0, u]] += mine[0, 0, u]
    for u in range(block_count):
        slot = own[0, 0, low_met[0, 0, u]]
        if plan.balanced:
            slot = jnp.where(turned, out_met[0, 0, u], slot)
        tiles[slot] += met[0, 0, u]
    c, b = lax.axis_index("cube"), lax.axis_index("blk")
    for ref, (straight, crossed) in zip(row_refs, row_offsets):
        at = lax.bitwise_xor(c, jnp.where(turned, jnp.int32(crossed), jnp.int32(straight)))
        left[pl.ds(pl.multiple_of(at * part_rows, part_rows), part_rows), :] = ref[...]
    for ref, offset in zip(col_refs, col_offsets):
        at = lax.bitwise_xor(b, jnp.int32(offset))
        right[pl.ds(pl.multiple_of(at * part_rows, part_rows), part_rows), :] = ref[...]
    size = tiles.shape[1]
    across = right.shape[0] // size

    @pl.loop(0, left.shape[0] // size)
    def _(i):
        panel = left[pl.ds(pl.multiple_of(i * size, size), size), :]
        for j in range(across):
            product = lax.dot_general(
                panel,
                right[j * size : (j + 1) * size, :],
                (((1,), (1,)), ((), ())),
                precision=lax.Precision.HIGHEST,
                preferred_element_type=jnp.float32,
            )
            part[pl.ds(pl.multiple_of(i * size, size), size), j * size : (j + 1) * size] = (
                tiles[i * across + j] - product
            )


def last_kernel(plan, block_count, out_other, part, got, result, *scratch):
    size = got.shape[-1]
    across = result.shape[1] // size
    tiles = got
    if not plan.balanced:
        tiles = scratch[0]
        tiles[...] = jnp.zeros_like(tiles)
        for u in range(block_count):
            tiles[out_other[0, 0, u]] += got[u]
    for t in range(tiles.shape[0]):
        i, j = t // across, t % across
        at = (slice(i * size, (i + 1) * size), slice(j * size, (j + 1) * size))
        result[at] = part[at] + tiles[t]


def local(updates, pivot_panel, map_low, map_own, map_out):
    block_count, size = updates.shape[2], updates.shape[3]
    part_rows, depth = pivot_panel.shape
    row_count = lax.axis_size("cube") * part_rows
    col_count = lax.axis_size("blk") * part_rows
    tile_count = row_count // size * (col_count // size)
    plan = Plan(tile_count, block_count)
    f32 = jnp.float32

    met = plan.swap(updates, 0)
    low_met, out_met = plan.swap(map_low, 0), plan.swap(map_out, 0)
    own_other, out_other = plan.swap(map_own, 1), plan.swap(map_out, 1)
    out_far = plan.swap(out_met, 1)

    s0, s1 = (plan.offset(0, 0), plan.offset(1, 0)), (plan.offset(0, 1), plan.offset(1, 1))
    near = plan.swap(pivot_panel, 0)
    row_panels = [pivot_panel, near, plan.swap(pivot_panel, 1), plan.swap(near, 1)]
    row_offsets = [(0, 0), s0, s1, (s0[0] ^ s1[0], s0[1] ^ s1[1])]
    for offset in [1 << k for k in range(plan.cubes.bit_length() - 1)]:
        if offset not in (plan.low, plan.up):
            row_panels += [flipped(p, "cube", offset) for p in row_panels]
            row_offsets += [(a ^ offset, d ^ offset) for a, d in row_offsets]
    col_offsets = list(range(0, plan.blks, 2))
    col_panels = [pivot_panel if o == 0 else flipped(pivot_panel, "blk", o) for o in col_offsets]
    col_panels += [flipped(p, "blk", 1) for p in col_panels]
    col_offsets += [o + 1 for o in col_offsets]

    sent = pl.pallas_call(
        functools.partial(send_kernel, plan, block_count),
        out_shape=jax.ShapeDtypeStruct((block_count, size, size), f32),
        in_specs=[SMEM] * 5 + [VMEM] * 2,
        out_specs=VMEM,
        compiler_params=pltpu.CompilerParams(vmem_limit_bytes=16 << 20),
        cost_estimate=pl.CostEstimate(flops=1 << 18, bytes_accessed=3 << 19, transcendentals=0),
        name="send",
    )(map_low, map_out, low_met, own_other, out_far, updates, met)
    got = plan.swap(sent, 1)

    part = pl.pallas_call(
        functools.partial(part_kernel, plan, block_count, row_offsets, col_offsets),
        out_shape=jax.ShapeDtypeStruct((row_count, col_count), f32),
        in_specs=[SMEM] * 3 + [VMEM] * (2 + len(row_panels) + len(col_panels)),
        out_specs=VMEM,
        scratch_shapes=[
            pltpu.VMEM((tile_count, size, size), f32),
            pltpu.VMEM((row_count, depth), f32),
            pltpu.VMEM((col_count, depth), f32),
        ],
        compiler_params=pltpu.CompilerParams(vmem_limit_bytes=40 << 20),
        cost_estimate=pl.CostEstimate(
            flops=12 * row_count * col_count * depth, bytes_accessed=1 << 21, transcendentals=0
        ),
        name="part",
    )(map_own, low_met, out_met, updates, met, *row_panels, *col_panels)

    result = pl.pallas_call(
        functools.partial(last_kernel, plan, block_count),
        out_shape=jax.ShapeDtypeStruct((row_count, col_count), f32),
        in_specs=[SMEM, VMEM, VMEM],
        out_specs=VMEM,
        scratch_shapes=[] if plan.balanced else [pltpu.VMEM((tile_count, size, size), f32)],
        compiler_params=pltpu.CompilerParams(vmem_limit_bytes=40 << 20),
        cost_estimate=pl.CostEstimate(flops=1 << 18, bytes_accessed=3 << 19, transcendentals=0),
        name="last",
    )(out_other, part, got)
    return result.reshape(lax.axis_size("cube"), 1, part_rows, col_count)


def solution(mesh):
    placed = (
        P("cube", "blk", None, None, None),
        P(("cube", "blk"), None),
        P("cube", "blk", None),
        P("cube", "blk", None),
        P("cube", "blk", None),
    )
    return jax.shard_map(
        local, mesh=mesh, in_specs=placed, out_specs=P(None, "blk", None, "cube"), check_vma=False
    )
```

time: 55 us -> 39 us (0.71)
  blocking collectives: 31.1 us -> 0 us
  starting transfers between devices: 5.42 us -> 20 us
  matrix products: 4.21 us -> 0 us
  Pallas kernels: 0 us -> 4.04 us
  local copies, waits for them, and re-layouts: 1.77 us -> 2.36 us
    all_gather x2 -> x0, blocking collectives: 31.1 us -> none  [the longest x1 15.8 us: local(): lax.all_gather(pivot_panel, 'blk', axis=0, tiled=True)]
    ppermute x3 -> x17, starting transfers between devices: 5.42 us -> 20 us  [the longest x10 15 us: swap(): return lax.ppermute(shard, AXES, pairs)]
    dot_general x4 -> x0, matrix products: 4.21 us -> none  [the longest x3 2.79 us: scatter_slots(): jnp.dot(one_hot(targets, classes).T, blocks, precision=exact_mode, prefer...]
    pallas_call x0 -> x3, Pallas kernels: none -> 4.04 us  [the longest x1 1.91 us: local(): pl.pallas_call(functools.partial(part_kernel, plan, block_count, row_offs...]
    unnamed x11 -> x12, local copies, waits for them, and re-layouts: 1.42 us -> 2.36 us
    ppermute x3 -> x17, waiting for transfers between devices: 11.9 us -> 12.4 us  [the longest x10 8.88 us: swap(): return lax.ppermute(shard, AXES, pairs)]
  transfers between devices with their start and end apart: 3 -> 17, of which waited for: 1 -> 6; matrix products, arithmetic and copies ran while one was open for 0% -> 0% of each run, Pallas kernels for 0% -> 5%
where the time goes in v1:
time: 39 us; the launch traced here: 38.8 us
  starting transfers between devices  20 us (51%)
  waiting for transfers between devices  12.4 us (32%)
  Pallas kernels  4.04 us (10%)
  local copies, waits for them, and re-layouts  2.36 us (6%)
    ppermute x10, starting transfers between devices, swap(): return lax.ppermute(shard, AXES, pairs)  15 us
    ppermute x10, waiting for transfers between devices, swap(): return lax.ppermute(shard, AXES, pairs)  8.88 us
    ppermute x7, starting transfers between devices, flipped(): lax.ppermute(shard, axis, [(i, i ^ offset) for i in range(lax.axis_size(a...  4.97 us
    ppermute x7, waiting for transfers between devices, flipped(): lax.ppermute(shard, axis, [(i, i ^ offset) for i in range(lax.axis_size(a...  3.49 us
    unnamed x12, local copies, waits for them, and re-layouts  2.36 us
    pallas_call x1, Pallas kernels, local(): pl.pallas_call(functools.partial(part_kernel, plan, block_count, row_offs...  1.91 us
    pallas_call x1, Pallas kernels, local(): pl.pallas_call(functools.partial(last_kernel, plan, block_count), out_sha...  1.39 us
  transfers between devices with their start and end apart: 17, of which 6 were waited for; matrix products, arithmetic and copies ran while one was open for 0% of the time, Pallas kernels for 5%

profile of v1, /device:TPU:0, one launch (start us, length us, event | category | flops | bytes accessed | tf_op | source)
XLA Modules:
  0.0 38.8 jit_solution(12757184243515658330)
XLA Ops:
  0.0 2.9 %collective-permute-start.3 = (f32[1,1,8,128,128]{4,3,2,1,0:T(8,128)}, f32[1,1,8,128,128]{4,3,2,1,0:T(8,128)S(1)}, u32[]{:S(2)}, u32[]{:S(2)}) collective-permute-start(f32[1,1,8,128,128]{4,3,2,1,0:T(8,128)} %mine.1), channel_id=1, source_target_pairs={{0,8},{1,17},{2,10},{3,19},{4,12},{5,21},{6,14},{7,23},{8,0},{9,25... | collective-permute-start | bytes 1572872 | tf_op jit(solution)/shard_map/ppermute | solution.py:34
  2.9 0.0 collective-permute-start.1
  3.0 2.0 %collective-permute-start.2 = (s32[1,1,8]{2,1,0:T(1,128)}, s32[1,1,8]{2,1,0:T(1,128)S(1)}, u32[]{:S(2)}, u32[]{:S(2)}) collective-permute-start(s32[1,1,8]{2,1,0:T(1,128)} %out.1), channel_id=1, source_target_pairs={{0,8},{1,17},{2,10},{3,19},{4,12},{5,21},{6,14},{7,23},{8,0},{9,25... | collective-permute-start | bytes 104 | tf_op jit(solution)/shard_map/ppermute | solution.py:34
  5.0 1.5 %collective-permute-start.14 = (s32[1,1,8]{2,1,0:T(1,128)}, s32[1,1,8]{2,1,0:T(1,128)S(1)}, u32[]{:S(2)}, u32[]{:S(2)}) collective-permute-start(s32[1,1,8]{2,1,0:T(1,128)} %own.1), channel_id=1, source_target_pairs={{0,16},{1,9},{2,18},{3,11},{4,20},{5,13},{6,22},{7,15},{8,24},{9,1... | collective-permute-start | bytes 104 | tf_op jit(solution)/shard_map/ppermute | solution.py:34
  6.5 3.9 %collective-permute-done.2.out_met = s32[1,1,8]{2,1,0:T(1,128)S(1)} collective-permute-done((s32[1,1,8]{2,1,0:T(1,128)}, s32[1,1,8]{2,1,0:T(1,128)S(1)}, u32[]{:S(2)}, u32[]{:S(2)}) %collective-permute-start.2) | collective-permute-done | bytes 64 | tf_op jit(solution)/shard_map/ppermute | solution.py:34
  10.4 2.1 %collective-permute-start.15 = (s32[1,1,8]{2,1,0:T(1,128)S(1)}, s32[1,1,8]{2,1,0:T(1,128)S(1)}, u32[]{:S(2)}, u32[]{:S(2)}) collective-permute-start(s32[1,1,8]{2,1,0:T(1,128)S(1)} %collective-permute-done.2.out_met), channel_id=1, source_target_pairs={{0,16},{1,9},{2,18},{3,11},{4,20},{5,13},{6,22},{7,15},{8,24},{9,1... | collective-permute-start | bytes 104 | tf_op jit(solution)/shard_map/ppermute | solution.py:34
  12.4 0.0 collective-permute-done.1.low_met
  12.4 0.0 collective-permute-done.14.own_other
  12.4 1.5 %collective-permute-done.15.out_far = s32[1,1,8]{2,1,0:T(1,128)S(1)} collective-permute-done((s32[1,1,8]{2,1,0:T(1,128)S(1)}, s32[1,1,8]{2,1,0:T(1,128)S(1)}, u32[]{:S(2)}, u32[]{:S(2)}) %collective-permute-start.15) | collective-permute-done | bytes 64 | tf_op jit(solution)/shard_map/ppermute | solution.py:34
  13.9 0.0 collective-permute-done.3.refs_1_.met
  14.0 0.0 copy-start
  14.0 1.0 %copy-done = f32[1,1,8,128,128]{4,3,2,1,0:T(8,128)S(1)} copy-done((f32[1,1,8,128,128]{4,3,2,1,0:T(8,128)S(1)}, f32[1,1,8,128,128]{4,3,2,1,0:T(8,128)}, u32[]{:S(2)}) %copy-start) | copy-done | bytes 524312
  15.0 0.0 copy-start.3
  15.0 0.7 %copy-done.3 = s32[1,1,8]{2,1,0:T(1,128)S(1)} copy-done((s32[1,1,8]{2,1,0:T(1,128)S(1)}, s32[1,1,8]{2,1,0:T(1,128)}, u32[]{:S(2)}) %copy-start.3) | copy-done | bytes 56
  15.7 0.0 copy-start.5
  15.7 0.7 %copy-done.5 = s32[1,1,8]{2,1,0:T(1,128)S(1)} copy-done((s32[1,1,8]{2,1,0:T(1,128)S(1)}, s32[1,1,8]{2,1,0:T(1,128)}, u32[]{:S(2)}) %copy-start.5) | copy-done | bytes 56
  16.3 0.0 copy-start.2
  16.3 0.0 copy-start.1
  16.3 0.0 copy-start.4
  16.3 0.7 %send.1 = f32[8,128,128]{2,1,0:T(8,128)S(1)} custom-call(s32[1,1,8]{2,1,0:T(1,128)S(1)} %copy-done.3, s32[1,1,8]{2,1,0:T(1,128)S(1)} %copy-done.5, s32[1,1,8]{2,1,0:T(1,128)S(1)} %collective-permute-done.1.low_met, s32[1,1,8]{2,1,0:T(1,128)S(1)} %collective-permute-done.14.own_other, s32[1,1,8]{2,1,0:T(1,128)S(1)} %collective-permute-done.15.out_far, ...), custom_call_target="tpu_custom_call" | custom-call | flops 262144 | bytes 1572864 | tf_op jit(solution)/shard_map/send/pallas_call | solution.py:143
  17.1 2.1 %collective-permute-start.16 = (f32[8,128,128]{2,1,0:T(8,128)S(1)}, f32[8,128,128]{2,1,0:T(8,128)S(1)}, u32[]{:S(2)}, u32[]{:S(2)}) collective-permute-start(f32[8,128,128]{2,1,0:T(8,128)S(1)} %send.1), channel_id=1, source_target_pairs={{0,16},{1,9},{2,18},{3,11},{4,20},{5,13},{6,22},{7,15},{8,24},{9,1... | collective-permute-start | bytes 1572872 | tf_op jit(solution)/shard_map/ppermute | solution.py:34
  19.1 0.0 copy-done.2
  19.1 1.6 %collective-permute-start.7 = (f32[64,256]{1,0:T(8,128)S(1)}, f32[64,256]{1,0:T(8,128)S(1)}, u32[]{:S(2)}, u32[]{:S(2)}) collective-permute-start(f32[64,256]{1,0:T(8,128)S(1)} %copy-done.2), channel_id=1, source_target_pairs={{0,2},{1,3},{2,0},{3,1},{4,6},{5,7},{6,4},{7,5},{8,10},{9,11},{10,... | collective-permute-start | bytes 196616 | tf_op jit(solution)/shard_map/ppermute | solution.py:41
  20.7 2.6 %collective-permute-start.8 = (f32[64,256]{1,0:T(8,128)S(1)}, f32[64,256]{1,0:T(8,128)S(1)}, u32[]{:S(2)}, u32[]{:S(2)}) collective-permute-start(f32[64,256]{1,0:T(8,128)S(1)} %copy-done.2), channel_id=1, source_target_pairs={{0,4},{1,5},{2,6},{3,7},{4,0},{5,1},{6,2},{7,3},{8,12},{9,13},{10,... | collective-permute-start | bytes 196616 | tf_op jit(solution)/shard_map/ppermute | solution.py:41
  23.3 0.2 collective-permute-start.9
  23.5 1.5 %collective-permute-start.4 = (f32[64,256]{1,0:T(8,128)S(1)}, f32[64,256]{1,0:T(8,128)S(1)}, u32[]{:S(2)}, u32[]{:S(2)}) collective-permute-start(f32[64,256]{1,0:T(8,128)S(1)} %copy-done.2), channel_id=1, source_target_pairs={{0,8},{1,17},{2,10},{3,19},{4,12},{5,21},{6,14},{7,23},{8,0},{9,25... | collective-permute-start | bytes 196616 | tf_op jit(solution)/shard_map/ppermute | solution.py:34
  25.0 0.0 collective-permute-done.7.refs_7_
  25.0 0.0 collective-permute-start.10
  25.0 1.9 %collective-permute-done.8.refs_8_ = f32[64,256]{1,0:T(8,128)S(1)} collective-permute-done((f32[64,256]{1,0:T(8,128)S(1)}, f32[64,256]{1,0:T(8,128)S(1)}, u32[]{:S(2)}, u32[]{:S(2)}) %collective-permute-start.8) | collective-permute-done | bytes 65568 | tf_op jit(solution)/shard_map/ppermute | solution.py:41
  26.9 0.9 %collective-permute-start.5 = (f32[64,256]{1,0:T(8,128)S(1)}, f32[64,256]{1,0:T(8,128)S(1)}, u32[]{:S(2)}, u32[]{:S(2)}) collective-permute-start(f32[64,256]{1,0:T(8,128)S(1)} %copy-done.2), channel_id=1, source_target_pairs={{0,16},{1,9},{2,18},{3,11},{4,20},{5,13},{6,22},{7,15},{8,24},{9,1... | collective-permute-start | bytes 196616 | tf_op jit(solution)/shard_map/ppermute | solution.py:34
  27.8 1.6 %collective-permute-done.9.refs_9_ = f32[64,256]{1,0:T(8,128)S(1)} collective-permute-done((f32[64,256]{1,0:T(8,128)S(1)}, f32[64,256]{1,0:T(8,128)S(1)}, u32[]{:S(2)}, u32[]{:S(2)}) %collective-permute-start.9) | collective-permute-done | bytes 65568 | tf_op jit(solution)/shard_map/ppermute | solution.py:41
  29.4 0.0 collective-permute-start.11
  29.4 0.0 collective-permute-done.4.refs_3_
  29.4 0.5 %collective-permute-start.12 = (f32[64,256]{1,0:T(8,128)S(1)}, f32[64,256]{1,0:T(8,128)S(1)}, u32[]{:S(2)}, u32[]{:S(2)}) collective-permute-start(f32[64,256]{1,0:T(8,128)S(1)} %collective-permute-done.8.refs_8_), channel_id=1, source_target_pairs={{0,1},{1,0},{2,3},{3,2},{4,5},{5,4},{6,7},{7,6},{8,9},{9,8},{10,11... | collective-permute-start | bytes 196616 | tf_op jit(solution)/shard_map/ppermute | solution.py:41
  29.9 0.0 collective-permute-done.10.refs_10_
  29.9 0.1 collective-permute-start.13
  30.0 1.2 %collective-permute-done.5.refs_4_ = f32[64,256]{1,0:T(8,128)S(1)} collective-permute-done((f32[64,256]{1,0:T(8,128)S(1)}, f32[64,256]{1,0:T(8,128)S(1)}, u32[]{:S(2)}, u32[]{:S(2)}) %collective-permute-start.5) | collective-permute-done | bytes 65568 | tf_op jit(solution)/shard_map/ppermute | solution.py:34
  31.2 0.9 %collective-permute-start.6 = (f32[64,256]{1,0:T(8,128)S(1)}, f32[64,256]{1,0:T(8,128)S(1)}, u32[]{:S(2)}, u32[]{:S(2)}) collective-permute-start(f32[64,256]{1,0:T(8,128)S(1)} %collective-permute-done.4.refs_3_), channel_id=1, source_target_pairs={{0,16},{1,9},{2,18},{3,11},{4,20},{5,13},{6,22},{7,15},{8,24},{9,1... | collective-permute-start | bytes 196616 | tf_op jit(solution)/shard_map/ppermute | solution.py:34
  32.1 0.0 collective-permute-done.11.refs_11_
  32.1 1.2 %collective-permute-start = (s32[1,1,8]{2,1,0:T(1,128)S(1)}, s32[1,1,8]{2,1,0:T(1,128)S(1)}, u32[]{:S(2)}, u32[]{:S(2)}) collective-permute-start(s32[1,1,8]{2,1,0:T(1,128)S(1)} %copy-done.5), channel_id=1, source_target_pairs={{0,16},{1,9},{2,18},{3,11},{4,20},{5,13},{6,22},{7,15},{8,24},{9,1... | collective-permute-start | bytes 104 | tf_op jit(solution)/shard_map/ppermute | solution.py:34
  33.2 0.0 collective-permute-done.12.refs_12_
  33.2 0.0 collective-permute-done.13.refs_13_
  33.2 2.2 %collective-permute-done.6.refs_5_ = f32[64,256]{1,0:T(8,128)S(1)} collective-permute-done((f32[64,256]{1,0:T(8,128)S(1)}, f32[64,256]{1,0:T(8,128)S(1)}, u32[]{:S(2)}, u32[]{:S(2)}) %collective-permute-start.6) | collective-permute-done | bytes 65568 | tf_op jit(solution)/shard_map/ppermute | solution.py:34
  35.5 0.0 copy-done.1
  35.5 0.0 copy-done.4
  35.5 1.9 %part.1 = f32[256,512]{1,0:T(8,128)S(1)} custom-call(s32[1,1,8]{2,1,0:T(1,128)S(1)} %copy-done.4, s32[1,1,8]{2,1,0:T(1,128)S(1)} %collective-permute-done.1.low_met, s32[1,1,8]{2,1,0:T(1,128)S(1)} %collective-permute-done.2.out_met, f32[1,1,8,128,128]{4,3,2,1,0:T(8,128)S(1)} %copy-done.1, f32[1,1,8,128,128]{4,3,2,1,0:T(8,128)S(1)} %collective-permute-done.3.refs_1_.met, ...), custom_call_target="tpu_custom_call" | custom-call | flops 402653184 | bytes 2097152 | tf_op jit(solution)/shard_map/part/pallas_call | solution.py:154
  37.4 0.0 collective-permute-done.out_other
  37.4 0.0 collective-permute-done.16.got
  37.4 1.4 %last.1 = f32[256,512]{1,0:T(8,128)} custom-call(s32[1,1,8]{2,1,0:T(1,128)S(1)} %collective-permute-done.out_other, f32[256,512]{1,0:T(8,128)S(1)} %part.1, f32[8,128,128]{2,1,0:T(8,128)S(1)} %collective-permute-done.16.got), custom_call_target="tpu_custom_call" | custom-call | flops 262144 | bytes 1572864 | tf_op jit(solution)/shard_map/last/pallas_call | solution.py:171
Async XLA Ops:
  0.0 14.0 %collective-permute-start.3 = (f32[1,1,8,128,128]{4,3,2,1,0:T(8,128)}, f32[1,1,8,128,128]{4,3,2,1,0:T(8,128)S(1)}, u32[]{:S(2)}, u32[]{:S(2)}) collective-permute-start(f32[1,1,8,128,128]{4,3,2,1,0:T(8,128)} %mine.1), channel_id=1, source_target_pairs={{0,8},{1,17},{2,10},{3,19},{4,12},{5,21},{6,14},{7,23},{8,0},{9,25... | collective-permute-start | bytes 1572872 | tf_op jit(solution)/shard_map/ppermute | solution.py:34
  2.9 9.5 %collective-permute-start.1 = (s32[1,1,8]{2,1,0:T(1,128)}, s32[1,1,8]{2,1,0:T(1,128)S(1)}, u32[]{:S(2)}, u32[]{:S(2)}) collective-permute-start(s32[1,1,8]{2,1,0:T(1,128)} %low.1), channel_id=1, source_target_pairs={{0,8},{1,17},{2,10},{3,19},{4,12},{5,21},{6,14},{7,23},{8,0},{9,25... | collective-permute-start | bytes 104 | tf_op jit(solution)/shard_map/ppermute | solution.py:34
  3.0 7.4 %collective-permute-start.2 = (s32[1,1,8]{2,1,0:T(1,128)}, s32[1,1,8]{2,1,0:T(1,128)S(1)}, u32[]{:S(2)}, u32[]{:S(2)}) collective-permute-start(s32[1,1,8]{2,1,0:T(1,128)} %out.1), channel_id=1, source_target_pairs={{0,8},{1,17},{2,10},{3,19},{4,12},{5,21},{6,14},{7,23},{8,0},{9,25... | collective-permute-start | bytes 104 | tf_op jit(solution)/shard_map/ppermute | solution.py:34
  5.0 7.5 %collective-permute-start.14 = (s32[1,1,8]{2,1,0:T(1,128)}, s32[1,1,8]{2,1,0:T(1,128)S(1)}, u32[]{:S(2)}, u32[]{:S(2)}) collective-permute-start(s32[1,1,8]{2,1,0:T(1,128)} %own.1), channel_id=1, source_target_pairs={{0,16},{1,9},{2,18},{3,11},{4,20},{5,13},{6,22},{7,15},{8,24},{9,1... | collective-permute-start | bytes 104 | tf_op jit(solution)/shard_map/ppermute | solution.py:34
  10.4 3.6 %collective-permute-start.15 = (s32[1,1,8]{2,1,0:T(1,128)S(1)}, s32[1,1,8]{2,1,0:T(1,128)S(1)}, u32[]{:S(2)}, u32[]{:S(2)}) collective-permute-start(s32[1,1,8]{2,1,0:T(1,128)S(1)} %collective-permute-done.2.out_met), channel_id=1, source_target_pairs={{0,16},{1,9},{2,18},{3,11},{4,20},{5,13},{6,22},{7,15},{8,24},{9,1... | collective-permute-start | bytes 104 | tf_op jit(solution)/shard_map/ppermute | solution.py:34
  14.0 1.0 %copy-start = (f32[1,1,8,128,128]{4,3,2,1,0:T(8,128)S(1)}, f32[1,1,8,128,128]{4,3,2,1,0:T(8,128)}, u32[]{:S(2)}) copy-start(f32[1,1,8,128,128]{4,3,2,1,0:T(8,128)} %mine.1) | copy-start | bytes 1572868
  15.0 0.7 %copy-start.3 = (s32[1,1,8]{2,1,0:T(1,128)S(1)}, s32[1,1,8]{2,1,0:T(1,128)}, u32[]{:S(2)}) copy-start(s32[1,1,8]{2,1,0:T(1,128)} %low.1) | copy-start | bytes 100
  15.7 0.7 %copy-start.5 = (s32[1,1,8]{2,1,0:T(1,128)S(1)}, s32[1,1,8]{2,1,0:T(1,128)}, u32[]{:S(2)}) copy-start(s32[1,1,8]{2,1,0:T(1,128)} %out.1) | copy-start | bytes 100
  16.3 2.8 %copy-start.2 = (f32[64,256]{1,0:T(8,128)S(1)}, f32[64,256]{1,0:T(8,128)}, u32[]{:S(2)}) copy-start(f32[64,256]{1,0:T(8,128)} %refs_6_.1) | copy-start | bytes 196612
  16.3 19.2 %copy-start.1 = (f32[1,1,8,128,128]{4,3,2,1,0:T(8,128)S(1)}, f32[1,1,8,128,128]{4,3,2,1,0:T(8,128)}, u32[]{:S(2)}) copy-start(f32[1,1,8,128,128]{4,3,2,1,0:T(8,128)} %mine.1) | copy-start | bytes 1572868
  16.3 19.2 %copy-start.4 = (s32[1,1,8]{2,1,0:T(1,128)S(1)}, s32[1,1,8]{2,1,0:T(1,128)}, u32[]{:S(2)}) copy-start(s32[1,1,8]{2,1,0:T(1,128)} %own.1) | copy-start | bytes 100
  17.1 20.3 %collective-permute-start.16 = (f32[8,128,128]{2,1,0:T(8,128)S(1)}, f32[8,128,128]{2,1,0:T(8,128)S(1)}, u32[]{:S(2)}, u32[]{:S(2)}) collective-permute-start(f32[8,128,128]{2,1,0:T(8,128)S(1)} %send.1), channel_id=1, source_target_pairs={{0,16},{1,9},{2,18},{3,11},{4,20},{5,13},{6,22},{7,15},{8,24},{9,1... | collective-permute-start | bytes 1572872 | tf_op jit(solution)/shard_map/ppermute | solution.py:34
  19.1 5.9 %collective-permute-start.7 = (f32[64,256]{1,0:T(8,128)S(1)}, f32[64,256]{1,0:T(8,128)S(1)}, u32[]{:S(2)}, u32[]{:S(2)}) collective-permute-start(f32[64,256]{1,0:T(8,128)S(1)} %copy-done.2), channel_id=1, source_target_pairs={{0,2},{1,3},{2,0},{3,1},{4,6},{5,7},{6,4},{7,5},{8,10},{9,11},{10,... | collective-permute-start | bytes 196616 | tf_op jit(solution)/shard_map/ppermute | solution.py:41
  20.7 6.2 %collective-permute-start.8 = (f32[64,256]{1,0:T(8,128)S(1)}, f32[64,256]{1,0:T(8,128)S(1)}, u32[]{:S(2)}, u32[]{:S(2)}) collective-permute-start(f32[64,256]{1,0:T(8,128)S(1)} %copy-done.2), channel_id=1, source_target_pairs={{0,4},{1,5},{2,6},{3,7},{4,0},{5,1},{6,2},{7,3},{8,12},{9,13},{10,... | collective-permute-start | bytes 196616 | tf_op jit(solution)/shard_map/ppermute | solution.py:41
  23.3 6.1 %collective-permute-start.9 = (f32[64,256]{1,0:T(8,128)S(1)}, f32[64,256]{1,0:T(8,128)S(1)}, u32[]{:S(2)}, u32[]{:S(2)}) collective-permute-start(f32[64,256]{1,0:T(8,128)S(1)} %copy-done.2), channel_id=1, source_target_pairs={{0,6},{1,7},{2,4},{3,5},{4,2},{5,3},{6,0},{7,1},{8,14},{9,15},{10,... | collective-permute-start | bytes 196616 | tf_op jit(solution)/shard_map/ppermute | solution.py:41
  23.5 5.8 %collective-permute-start.4 = (f32[64,256]{1,0:T(8,128)S(1)}, f32[64,256]{1,0:T(8,128)S(1)}, u32[]{:S(2)}, u32[]{:S(2)}) collective-permute-start(f32[64,256]{1,0:T(8,128)S(1)} %copy-done.2), channel_id=1, source_target_pairs={{0,8},{1,17},{2,10},{3,19},{4,12},{5,21},{6,14},{7,23},{8,0},{9,25... | collective-permute-start | bytes 196616 | tf_op jit(solution)/shard_map/ppermute | solution.py:34
  25.0 4.9 %collective-permute-start.10 = (f32[64,256]{1,0:T(8,128)S(1)}, f32[64,256]{1,0:T(8,128)S(1)}, u32[]{:S(2)}, u32[]{:S(2)}) collective-permute-start(f32[64,256]{1,0:T(8,128)S(1)} %copy-done.2), channel_id=1, source_target_pairs={{0,1},{1,0},{2,3},{3,2},{4,5},{5,4},{6,7},{7,6},{8,9},{9,8},{10,11... | collective-permute-start | bytes 196616 | tf_op jit(solution)/shard_map/ppermute | solution.py:41
  26.9 4.3 %collective-permute-start.5 = (f32[64,256]{1,0:T(8,128)S(1)}, f32[64,256]{1,0:T(8,128)S(1)}, u32[]{:S(2)}, u32[]{:S(2)}) collective-permute-start(f32[64,256]{1,0:T(8,128)S(1)} %copy-done.2), channel_id=1, source_target_pairs={{0,16},{1,9},{2,18},{3,11},{4,20},{5,13},{6,22},{7,15},{8,24},{9,1... | collective-permute-start | bytes 196616 | tf_op jit(solution)/shard_map/ppermute | solution.py:34
  29.4 2.7 %collective-permute-start.11 = (f32[64,256]{1,0:T(8,128)S(1)}, f32[64,256]{1,0:T(8,128)S(1)}, u32[]{:S(2)}, u32[]{:S(2)}) collective-permute-start(f32[64,256]{1,0:T(8,128)S(1)} %collective-permute-done.7.refs_7_), channel_id=1, source_target_pairs={{0,1},{1,0},{2,3},{3,2},{4,5},{5,4},{6,7},{7,6},{8,9},{9,8},{10,11... | collective-permute-start | bytes 196616 | tf_op jit(solution)/shard_map/ppermute | solution.py:41
  29.4 3.8 %collective-permute-start.12 = (f32[64,256]{1,0:T(8,128)S(1)}, f32[64,256]{1,0:T(8,128)S(1)}, u32[]{:S(2)}, u32[]{:S(2)}) collective-permute-start(f32[64,256]{1,0:T(8,128)S(1)} %collective-permute-done.8.refs_8_), channel_id=1, source_target_pairs={{0,1},{1,0},{2,3},{3,2},{4,5},{5,4},{6,7},{7,6},{8,9},{9,8},{10,11... | collective-permute-start | bytes 196616 | tf_op jit(solution)/shard_map/ppermute | solution.py:41
  29.9 3.3 %collective-permute-start.13 = (f32[64,256]{1,0:T(8,128)S(1)}, f32[64,256]{1,0:T(8,128)S(1)}, u32[]{:S(2)}, u32[]{:S(2)}) collective-permute-start(f32[64,256]{1,0:T(8,128)S(1)} %collective-permute-done.9.refs_9_), channel_id=1, source_target_pairs={{0,1},{1,0},{2,3},{3,2},{4,5},{5,4},{6,7},{7,6},{8,9},{9,8},{10,11... | collective-permute-start | bytes 196616 | tf_op jit(solution)/shard_map/ppermute | solution.py:41
  31.2 4.3 %collective-permute-start.6 = (f32[64,256]{1,0:T(8,128)S(1)}, f32[64,256]{1,0:T(8,128)S(1)}, u32[]{:S(2)}, u32[]{:S(2)}) collective-permute-start(f32[64,256]{1,0:T(8,128)S(1)} %collective-permute-done.4.refs_3_), channel_id=1, source_target_pairs={{0,16},{1,9},{2,18},{3,11},{4,20},{5,13},{6,22},{7,15},{8,24},{9,1... | collective-permute-start | bytes 196616 | tf_op jit(solution)/shard_map/ppermute | solution.py:34
  32.1 5.3 %collective-permute-start = (s32[1,1,8]{2,1,0:T(1,128)S(1)}, s32[1,1,8]{2,1,0:T(1,128)S(1)}, u32[]{:S(2)}, u32[]{:S(2)}) collective-permute-start(s32[1,1,8]{2,1,0:T(1,128)S(1)} %copy-done.5), channel_id=1, source_target_pairs={{0,16},{1,9},{2,18},{3,11},{4,20},{5,13},{6,22},{7,15},{8,24},{9,1... | collective-permute-start | bytes 104 | tf_op jit(solution)/shard_map/ppermute | solution.py:34

commit v2 on v0

v2 whole, which is shorter than its diff:
```python
import functools

import jax
import jax.numpy as jnp
from jax import lax
from jax.experimental import pallas as pl
from jax.experimental.pallas import tpu as pltpu
from jax.sharding import PartitionSpec as P

AXES = ("cube", "blk")
VMEM = pl.BlockSpec(memory_space=pltpu.VMEM)
SMEM = pl.BlockSpec(memory_space=pltpu.SMEM)
ROW, COL = "row", "col"
LINES, LANES = 8, 128
LOW, OWN, OUT, OTHER = 0, 1, 2, 3
f32, i32 = jnp.float32, jnp.int32
COST = dict(hint=1 << 33, label=0, pack=0, pair=0, send=1 << 30, merge=0, part=1 << 31, last=0)


class Plan:
    def __init__(self, updates, pivot_panel):
        self.slots, self.size = updates.shape[2], updates.shape[3]
        self.part_rows, self.depth = pivot_panel.shape
        self.cubes, self.blks = lax.axis_size("cube"), lax.axis_size("blk")
        self.rows, self.cols = self.cubes * self.part_rows, self.blks * self.part_rows
        self.across = self.cols // self.size
        self.tiles = self.rows // self.size * self.across
        bit_count = self.cubes.bit_length() - 1
        self.low, self.up = 1 << (bit_count - 2), 1 << (bit_count - 1)
        self.balanced = self.tiles <= self.slots

    def offset(self, b, stage):
        turned = self.balanced and b % 2 == 1
        return self.up if turned == (stage == 0) else self.low

    def move(self, shard, even, odd):
        pairs = []
        for c in range(self.cubes):
            for b in range(self.blks):
                if (odd if b % 2 else even) is None:
                    continue
                dc, db = odd if b % 2 else even
                pairs.append((c * self.blks + b, (c ^ dc) * self.blks + (b ^ db)))
        return lax.ppermute(shard, AXES, pairs)

    def swap(self, shard, stage):
        return self.move(shard, (self.offset(0, stage), 0), (self.offset(1, stage), 0))

    def is_odd(self):
        return lax.rem(lax.axis_index("blk"), 2) == 1


def call(kernel, outs, in_specs, args, name, scratch=(), limit=8):
    return pl.pallas_call(
        kernel,
        out_shape=outs,
        in_specs=in_specs,
        out_specs=[VMEM] * len(outs) if isinstance(outs, list) else VMEM,
        scratch_shapes=list(scratch),
        compiler_params=pltpu.CompilerParams(vmem_limit_bytes=limit << 20),
        cost_estimate=pl.CostEstimate(flops=COST[name], bytes_accessed=0, transcendentals=0),
        name=name,
    )(*args)


def hint_kernel(mark):
    mark[...] = jnp.zeros_like(mark)


def label_kernel(n, mark, panel, low, own, out, labelled):
    labelled[0:n] = panel[...]
    labelled[n:] = jnp.zeros((LINES, labelled.shape[1]), f32)
    for line, ref in ((LOW, low), (OWN, own), (OUT, out)):
        labelled[n + line : n + line + 1, 0 : ref.shape[2]] = ref[0].astype(f32)


def pair_kernel(n, mark, own, other, joined):
    joined[0:n] = own[...]
    joined[n : 2 * n] = other[...]


def pack_kernel(n, after, labelled, other, panels, maps):
    panels[0:n] = labelled[0:n]
    panels[n : 2 * n] = other[0:n]
    maps[...] = jnp.zeros_like(maps)
    maps[0:3] = labelled[n : n + 3, 0:LANES].astype(i32)
    maps[3:6] = other[n : n + 3, 0:LANES].astype(i32)


def merge_kernel(n, after, also, along, next_to, joined):
    joined[0 : 2 * n] = along[...]
    joined[2 * n : 3 * n] = next_to[...]


def send_kernel(plan, maps, maps_met, mine, met, sent):
    if not plan.balanced:
        sent[...] = mine[0, 0]
        for u in range(plan.slots):
            sent[maps_met[LOW, u]] += met[0, 0, u]
        return
    odd = plan.is_odd()
    sent[...] = jnp.zeros_like(sent)
    for u in range(plan.slots):
        slot = jnp.where(odd, maps[OTHER + OWN, maps[LOW, u]], maps[OUT, u])
        sent[slot] += mine[0, 0, u]
    for u in range(plan.slots):
        slot = maps_met[LOW, u]
        slot = jnp.where(odd, maps_met[OTHER + OUT, slot], maps[OUT, slot])
        sent[slot] += met[0, 0, u]


def part_kernel(plan, places, maps, maps_met, mine, met, *refs):
    part, tiles, left, right = refs[-4:]
    n, size = plan.part_rows, plan.size
    odd = plan.is_odd()
    tiles[...] = jnp.zeros_like(tiles)
    for u in range(plan.slots):
        tiles[maps[OWN, u]] += mine[0, 0, u]
    for u in range(plan.slots):
        slot = maps[OWN, maps_met[LOW, u]]
        if plan.balanced:
            slot = jnp.where(odd, maps_met[OUT, u], slot)
        tiles[slot] += met[0, 0, u]

    def lay(parity):
        for ref, chunks in zip(refs, places[parity]):
            for k, (kind, offset) in ((k, place) for k, chunk in enumerate(chunks) for place in chunk):
                to, me = (left, lax.axis_index("cube")) if kind == ROW else (right, lax.axis_index("blk"))
                at = lax.bitwise_xor(me, i32(offset))
                to[pl.ds(pl.multiple_of(at * n, n), n), :] = ref[k * n : (k + 1) * n]

    if places[0] == places[1]:
        lay(0)
    else:
        pl.when(jnp.logical_not(odd))(functools.partial(lay, 0))
        pl.when(odd)(functools.partial(lay, 1))

    @pl.loop(0, plan.rows // size)
    def _(i):
        panel = left[pl.ds(pl.multiple_of(i * size, size), size), :]
        for j in range(plan.across):
            product = lax.dot_general(
                panel,
                right[j * size : (j + 1) * size, :],
                (((1,), (1,)), ((), ())),
                precision=lax.Precision.HIGHEST,
                preferred_element_type=f32,
            )
            part[pl.ds(pl.multiple_of(i * size, size), size), j * size : (j + 1) * size] = (
                tiles[i * plan.across + j] - product
            )


def last_kernel(plan, *refs):
    size, across = plan.size, plan.across
    if plan.balanced:
        part, tiles, result = refs
    else:
        maps, part, got, result, tiles = refs
        tiles[...] = jnp.zeros_like(tiles)
        for u in range(plan.slots):
            tiles[maps[OTHER + OUT, u]] += got[u]
    for t in range(plan.tiles):
        i, j = t // across, t % across
        at = (slice(i * size, (i + 1) * size), slice(j * size, (j + 1) * size))
        result[at] = part[at] + tiles[t]


def after(first, *then):
    return lax.optimization_barrier((first, *then))[1:]


def add_sent(plan, maps, updates, met):
    return call(
        functools.partial(send_kernel, plan),
        jax.ShapeDtypeStruct(updates.shape[2:], f32),
        [SMEM] * len(maps) + [VMEM] * 2,
        (*maps, updates, met),
        "send",
    )


def add_part(plan, places, maps, updates, met, panels):
    return call(
        functools.partial(part_kernel, plan, places),
        jax.ShapeDtypeStruct((plan.rows, plan.cols), f32),
        [SMEM] * 2 + [VMEM] * (2 + len(panels)),
        (*maps, updates, met, *panels),
        "part",
        [
            pltpu.VMEM((plan.tiles, plan.size, plan.size), f32),
            pltpu.VMEM((plan.rows, plan.depth), f32),
            pltpu.VMEM((plan.cols, plan.depth), f32),
        ],
        limit=40,
    )


def add_last(plan, maps, part, got):
    return call(
        functools.partial(last_kernel, plan),
        jax.ShapeDtypeStruct((plan.rows, plan.cols), f32),
        [SMEM] * len(maps) + [VMEM] * 2,
        (*maps, part, got),
        "last",
        [] if plan.balanced else [pltpu.VMEM((plan.tiles, plan.size, plan.size), f32)],
        limit=40,
    )


def any_mesh(plan, updates, pivot_panel, map_low, map_own, map_out):
    met = plan.swap(updates, 0)
    own_maps = jnp.concatenate([map_low[0], map_own[0], map_out[0]])
    maps = jnp.concatenate([own_maps, plan.swap(own_maps, 1)])
    maps_met = plan.swap(maps, 0)
    got = plan.swap(add_sent(plan, [maps, maps_met], updates, met), 1)
    panels, places = [pivot_panel], [[[(ROW, 0), (COL, 0)]]]
    for c in range(1, plan.cubes):
        panels.append(plan.move(pivot_panel, (c, 0), (c, 0)))
        places.append([[(ROW, c)]])
    for b in range(1, plan.blks):
        panels.append(plan.move(pivot_panel, (0, b), (0, b)))
        places.append([[(COL, b)]])
    part = add_part(plan, (places, places), (maps, maps_met), updates, met, panels)
    return add_last(plan, [] if plan.balanced else [maps], part, got)


def four_by_eight(plan, updates, pivot_panel, map_low, map_own, map_out):
    n, depth = plan.part_rows, plan.depth
    shape = jax.ShapeDtypeStruct
    sibling = plan.move(pivot_panel, (0, 1), (0, 1))
    met = plan.swap(updates, 0)
    mark = call(hint_kernel, shape((LINES, LANES), f32), [], (), "hint")
    labelled = call(
        functools.partial(label_kernel, n),
        shape((n + LINES, depth), f32),
        [VMEM] * 5,
        (mark, pivot_panel, map_low, map_own, map_out),
        "label",
    )
    other = plan.swap(labelled, 1)
    pair = call(
        functools.partial(pair_kernel, n),
        shape((2 * n, depth), f32),
        [VMEM] * 3,
        (labelled, pivot_panel, sibling),
        "pair",
    )
    along = plan.move(pair, (0, 4), (0, 6))
    panels, maps = call(
        functools.partial(pack_kernel, n),
        [shape((2 * n, depth), f32), shape((LINES, LANES), i32)],
        [VMEM] * 3,
        (pair, labelled, other),
        "pack",
    )
    maps_met = plan.swap(maps, 0)
    panels_met = plan.swap(panels, 0)

    sent = add_sent(plan, [maps, maps_met], updates, met)
    got = plan.swap(sent, 1)

    (panel_late,) = after(sent, pivot_panel)
    next_to = plan.move(panel_late, (0, 2), (0, 2))
    merged = call(
        functools.partial(merge_kernel, n),
        shape((3 * n, depth), f32),
        [VMEM] * 4,
        (sent, panels_met, along, next_to),
        "merge",
    )
    shared = plan.move(merged, (0, 1), (0, 1))
    (s0, s1), (o0, o1) = ((plan.offset(0, k), plan.offset(1, k)) for k in range(2))
    cols = lambda b: [[(COL, b)], [(COL, b ^ 1)]]
    rows = lambda s, o: [[[(ROW, o)]], [[(ROW, s)], [(ROW, s ^ o)]]]
    own = [[(ROW, 0), (COL, 0)], [(COL, 1)]]
    even = [own, *rows(s0, o0), cols(4) + [[(COL, 2)]], cols(7) + [[(COL, 3)]]]
    odd = [own, *rows(s1, o1), cols(6) + [[(COL, 2)]], cols(5) + [[(COL, 3)]]]
    panels = [pair, other, panels_met, merged, shared]
    part = add_part(plan, (even, odd), (maps, maps_met), updates, met, panels)
    return add_last(plan, [], part, got)


def local(updates, *rest):
    plan = Plan(updates, rest[0])
    known = plan.balanced and plan.cubes == 4 and plan.blks == 8
    result = (four_by_eight if known else any_mesh)(plan, updates, *rest)
    return result.reshape(plan.cubes, 1, plan.part_rows, plan.cols)


def solution(mesh):
    placed = (
        P("cube", "blk", None, None, None),
        P(("cube", "blk"), None),
        P("cube", "blk", None),
        P("cube", "blk", None),
        P("cube", "blk", None),
    )
    return jax.shard_map(
        local, mesh=mesh, in_specs=placed, out_specs=P(None, "blk", None, "cube"), check_vma=False
    )
```

time: 55 us -> 24.3 us (0.44)
  blocking collectives: 31.1 us -> 0 us
  starting transfers between devices: 5.42 us -> 12.5 us
  matrix products: 4.21 us -> 0 us
  waiting for transfers between devices: 11.9 us -> 7.79 us
  Pallas kernels: 0 us -> 3.76 us
  local copies, waits for them, and re-layouts: 1.77 us -> 0.02 us
    all_gather x2 -> x0, blocking collectives: 31.1 us -> none  [the longest x1 15.8 us: local(): lax.all_gather(pivot_panel, 'blk', axis=0, tiled=True)]
    ppermute x3 -> x9, starting transfers between devices: 5.42 us -> 12.5 us  [move(): return lax.ppermute(shard, AXES, pairs)]
    dot_general x4 -> x0, matrix products: 4.21 us -> none  [the longest x3 2.79 us: scatter_slots(): jnp.dot(one_hot(targets, classes).T, blocks, precision=exact_mode, prefer...]
    ppermute x3 -> x9, waiting for transfers between devices: 11.9 us -> 7.79 us  [move(): return lax.ppermute(shard, AXES, pairs)]
    pallas_call x0 -> x8, Pallas kernels: none -> 3.76 us  [call(): pl.pallas_call(kernel, out_shape=outs, in_specs=in_specs, out_specs=[VMEM...]
    unnamed x11 -> x10, local copies, waits for them, and re-layouts: 1.42 us -> 0.02 us
  transfers between devices with their start and end apart: 3 -> 9, of which waited for: 1 -> 5; matrix products, arithmetic and copies ran while one was open for 0% -> 0% of each run, Pallas kernels for 0% -> 9%
where the time goes in v2:
time: 24.3 us; the launch traced here: 24.2 us
  starting transfers between devices  12.5 us (51%)
  waiting for transfers between devices  7.79 us (32%)
  Pallas kernels  3.76 us (15%)
    ppermute x9, starting transfers between devices, move(): return lax.ppermute(shard, AXES, pairs)  12.5 us
    ppermute x9, waiting for transfers between devices, move(): return lax.ppermute(shard, AXES, pairs)  7.79 us
    pallas_call x8, Pallas kernels, call(): pl.pallas_call(kernel, out_shape=outs, in_specs=in_specs, out_specs=[VMEM...  3.76 us
  transfers between devices with their start and end apart: 9, of which 5 were waited for; matrix products, arithmetic and copies ran while one was open for 0% of the time, Pallas kernels for 9%

profile of v2, /device:TPU:0, one launch (start us, length us, event | category | flops | bytes accessed | tf_op | source)
XLA Modules:
  0.0 24.2 jit_solution(15203547641649271394)
XLA Ops:
  0.0 0.0 copy-start
  0.0 0.0 copy-start.3
  0.0 0.0 copy-start.2
  0.0 0.0 copy-start.1
  0.0 3.0 %collective-permute-start.3 = (f32[1,1,8,128,128]{4,3,2,1,0:T(8,128)}, f32[1,1,8,128,128]{4,3,2,1,0:T(8,128)S(1)}, u32[]{:S(2)}, u32[]{:S(2)}) collective-permute-start(f32[1,1,8,128,128]{4,3,2,1,0:T(8,128)} %mine.3), channel_id=1, source_target_pairs={{0,8},{1,17},{2,10},{3,19},{4,12},{5,21},{6,14},{7,23},{8,0},{9,25... | collective-permute-start | bytes 1572872 | tf_op jit(solution)/shard_map/ppermute | solution.py:44
  3.0 0.0 copy-done
  3.0 0.0 copy-done.3
  3.0 0.0 copy-done.2
  3.0 0.0 copy-done.1
  3.0 0.0 copy-start.4
  3.1 1.6 %collective-permute-start.1 = (f32[72,256]{1,0:T(8,128)S(1)}, f32[72,256]{1,0:T(8,128)S(1)}, u32[]{:S(2)}, u32[]{:S(2)}) collective-permute-start(f32[72,256]{1,0:T(8,128)S(1)} %label.1.mark.labelled), channel_id=1, source_target_pairs={{0,16},{1,9},{2,18},{3,11},{4,20},{5,13},{6,22},{7,15},{8,24},{9,1... | collective-permute-start | bytes 221192 | tf_op jit(solution)/shard_map/ppermute | solution.py:44
  4.7 0.0 collective-permute-start
  4.7 1.3 %collective-permute-done.other = f32[64,256]{1,0:T(8,128)S(1)} collective-permute-done((f32[64,256]{1,0:T(8,128)S(1)}, f32[64,256]{1,0:T(8,128)S(1)}, u32[]{:S(2)}, u32[]{:S(2)}) %collective-permute-start) | collective-permute-done | bytes 65568 | tf_op jit(solution)/shard_map/ppermute | solution.py:44
  5.9 2.4 %collective-permute-done.1.other.refs_1_ = f32[72,256]{1,0:T(8,128)S(1)} collective-permute-done((f32[72,256]{1,0:T(8,128)S(1)}, f32[72,256]{1,0:T(8,128)S(1)}, u32[]{:S(2)}, u32[]{:S(2)}) %collective-permute-start.1) | collective-permute-done | bytes 73760 | tf_op jit(solution)/shard_map/ppermute | solution.py:44
  8.4 0.8 %collective-permute-start.2 = (s32[8,128]{1,0:T(8,128)S(1)}, s32[8,128]{1,0:T(8,128)S(1)}, u32[]{:S(2)}, u32[]{:S(2)}) collective-permute-start(s32[8,128]{1,0:T(8,128)S(1)} %get-tuple-element.8.maps), channel_id=1, source_target_pairs={{0,8},{1,17},{2,10},{3,19},{4,12},{5,21},{6,14},{7,23},{8,0},{9,25... | collective-permute-start | bytes 12296 | tf_op jit(solution)/shard_map/ppermute | solution.py:44
  9.2 2.6 %collective-permute-start.5 = (f32[128,256]{1,0:T(8,128)S(1)}, f32[128,256]{1,0:T(8,128)S(1)}, u32[]{:S(2)}, u32[]{:S(2)}) collective-permute-start(f32[128,256]{1,0:T(8,128)S(1)} %pair.1.after.refs_0_), channel_id=1, source_target_pairs={{0,4},{1,7},{2,6},{3,5},{4,0},{5,3},{6,2},{7,1},{8,12},{9,15},{10,... | collective-permute-start | bytes 393224 | tf_op jit(solution)/shard_map/ppermute | solution.py:44
  11.8 1.3 %collective-permute-start.4 = (f32[128,256]{1,0:T(8,128)S(1)}, f32[128,256]{1,0:T(8,128)S(1)}, u32[]{:S(2)}, u32[]{:S(2)}) collective-permute-start(f32[128,256]{1,0:T(8,128)S(1)} %get-tuple-element.9), channel_id=1, source_target_pairs={{0,8},{1,17},{2,10},{3,19},{4,12},{5,21},{6,14},{7,23},{8,0},{9,25... | collective-permute-start | bytes 393224 | tf_op jit(solution)/shard_map/ppermute | solution.py:44
  13.0 0.0 collective-permute-done.2.maps_met
  13.0 0.0 collective-permute-done.3.met
  13.1 0.0 copy-done.4
  13.1 0.8 %send.1.after = f32[8,128,128]{2,1,0:T(8,128)S(1)} custom-call(s32[8,128]{1,0:T(8,128)S(1)} %get-tuple-element.8.maps, s32[8,128]{1,0:T(8,128)S(1)} %collective-permute-done.2.maps_met, f32[1,1,8,128,128]{4,3,2,1,0:T(8,128)S(1)} %copy-done.4, f32[1,1,8,128,128]{4,3,2,1,0:T(8,128)S(1)} %collective-permute-done.3.met), custom_call_target="tpu_custom_call" | custom-call | flops 1073741824 | tf_op jit(solution)/shard_map/send/pallas_call | solution.py:54
  13.9 1.6 %collective-permute-start.8 = (f32[8,128,128]{2,1,0:T(8,128)S(1)}, f32[8,128,128]{2,1,0:T(8,128)S(1)}, u32[]{:S(2)}, u32[]{:S(2)}) collective-permute-start(f32[8,128,128]{2,1,0:T(8,128)S(1)} %send.1.after), channel_id=1, source_target_pairs={{0,16},{1,9},{2,18},{3,11},{4,20},{5,13},{6,22},{7,15},{8,24},{9,1... | collective-permute-start | bytes 1572872 | tf_op jit(solution)/shard_map/ppermute | solution.py:44
  15.5 1.6 %collective-permute-start.6 = (f32[64,256]{1,0:T(8,128)S(1)}, f32[64,256]{1,0:T(8,128)S(1)}, u32[]{:S(2)}, u32[]{:S(2)}) collective-permute-start(f32[64,256]{1,0:T(8,128)S(1)} %copy-done), channel_id=1, source_target_pairs={{0,2},{1,3},{2,0},{3,1},{4,6},{5,7},{6,4},{7,5},{8,10},{9,11},{10,... | collective-permute-start | bytes 196616 | tf_op jit(solution)/shard_map/ppermute | solution.py:44
  17.1 0.0 collective-permute-done.5.along
  17.1 1.0 %collective-permute-done.4.also.refs_2_ = f32[128,256]{1,0:T(8,128)S(1)} collective-permute-done((f32[128,256]{1,0:T(8,128)S(1)}, f32[128,256]{1,0:T(8,128)S(1)}, u32[]{:S(2)}, u32[]{:S(2)}) %collective-permute-start.4) | collective-permute-done | bytes 131104 | tf_op jit(solution)/shard_map/ppermute | solution.py:44
  18.1 1.7 %collective-permute-done.6.next_to = f32[64,256]{1,0:T(8,128)S(1)} collective-permute-done((f32[64,256]{1,0:T(8,128)S(1)}, f32[64,256]{1,0:T(8,128)S(1)}, u32[]{:S(2)}, u32[]{:S(2)}) %collective-permute-start.6) | collective-permute-done | bytes 65568 | tf_op jit(solution)/shard_map/ppermute | solution.py:44
  19.8 0.1 collective-permute-start.7
  19.8 1.4 %collective-permute-done.7.refs_4_ = f32[192,256]{1,0:T(8,128)S(1)} collective-permute-done((f32[192,256]{1,0:T(8,128)S(1)}, f32[192,256]{1,0:T(8,128)S(1)}, u32[]{:S(2)}, u32[]{:S(2)}) %collective-permute-start.7) | collective-permute-done | bytes 196640 | tf_op jit(solution)/shard_map/ppermute | solution.py:44
  21.3 2.0 %part.1.refs_0_ = f32[256,512]{1,0:T(8,128)S(1)} custom-call(s32[8,128]{1,0:T(8,128)S(1)} %get-tuple-element.8.maps, s32[8,128]{1,0:T(8,128)S(1)} %collective-permute-done.2.maps_met, f32[1,1,8,128,128]{4,3,2,1,0:T(8,128)S(1)} %copy-done.4, f32[1,1,8,128,128]{4,3,2,1,0:T(8,128)S(1)} %collective-permute-done.3.met, f32[128,256]{1,0:T(8,128)S(1)} %pair.1.after.refs_0_, ...), custom_call_target="tpu_custom_call" | custom-call | flops 2147483648 | tf_op jit(solution)/shard_map/part/pallas_call | solution.py:54
  23.3 0.0 collective-permute-done.8.refs_1_
  23.3 0.9 %last.1 = f32[256,512]{1,0:T(8,128)} custom-call(f32[256,512]{1,0:T(8,128)S(1)} %part.1.refs_0_, f32[8,128,128]{2,1,0:T(8,128)S(1)} %collective-permute-done.8.refs_1_), custom_call_target="tpu_custom_call" | custom-call | tf_op jit(solution)/shard_map/last/pallas_call | solution.py:54
  (5 shorter events, 0.0 us)
Async XLA Ops:
  0.0 3.0 %copy-start = (f32[64,256]{1,0:T(8,128)S(1)}, f32[64,256]{1,0:T(8,128)}, u32[]{:S(2)}) copy-start(f32[64,256]{1,0:T(8,128)} %own.3) | copy-start | bytes 196612
  0.0 3.0 %copy-start.3 = (s32[1,1,8]{2,1,0:T(1,128)S(1)}, s32[1,1,8]{2,1,0:T(1,128)}, u32[]{:S(2)}) copy-start(s32[1,1,8]{2,1,0:T(1,128)} %out.1) | copy-start | bytes 100
  0.0 3.0 %copy-start.2 = (s32[1,1,8]{2,1,0:T(1,128)S(1)}, s32[1,1,8]{2,1,0:T(1,128)}, u32[]{:S(2)}) copy-start(s32[1,1,8]{2,1,0:T(1,128)} %own.2) | copy-start | bytes 100
  0.0 3.0 %copy-start.1 = (s32[1,1,8]{2,1,0:T(1,128)S(1)}, s32[1,1,8]{2,1,0:T(1,128)}, u32[]{:S(2)}) copy-start(s32[1,1,8]{2,1,0:T(1,128)} %low.1) | copy-start | bytes 100
  0.0 13.0 %collective-permute-start.3 = (f32[1,1,8,128,128]{4,3,2,1,0:T(8,128)}, f32[1,1,8,128,128]{4,3,2,1,0:T(8,128)S(1)}, u32[]{:S(2)}, u32[]{:S(2)}) collective-permute-start(f32[1,1,8,128,128]{4,3,2,1,0:T(8,128)} %mine.3), channel_id=1, source_target_pairs={{0,8},{1,17},{2,10},{3,19},{4,12},{5,21},{6,14},{7,23},{8,0},{9,25... | collective-permute-start | bytes 1572872 | tf_op jit(solution)/shard_map/ppermute | solution.py:44
  3.0 10.0 %copy-start.4 = (f32[1,1,8,128,128]{4,3,2,1,0:T(8,128)S(1)}, f32[1,1,8,128,128]{4,3,2,1,0:T(8,128)}, u32[]{:S(2)}) copy-start(f32[1,1,8,128,128]{4,3,2,1,0:T(8,128)} %mine.3) | copy-start | bytes 1572868
  3.1 5.3 %collective-permute-start.1 = (f32[72,256]{1,0:T(8,128)S(1)}, f32[72,256]{1,0:T(8,128)S(1)}, u32[]{:S(2)}, u32[]{:S(2)}) collective-permute-start(f32[72,256]{1,0:T(8,128)S(1)} %label.1.mark.labelled), channel_id=1, source_target_pairs={{0,16},{1,9},{2,18},{3,11},{4,20},{5,13},{6,22},{7,15},{8,24},{9,1... | collective-permute-start | bytes 221192 | tf_op jit(solution)/shard_map/ppermute | solution.py:44
  4.7 1.3 %collective-permute-start = (f32[64,256]{1,0:T(8,128)S(1)}, f32[64,256]{1,0:T(8,128)S(1)}, u32[]{:S(2)}, u32[]{:S(2)}) collective-permute-start(f32[64,256]{1,0:T(8,128)S(1)} %copy-done), channel_id=1, source_target_pairs={{0,1},{1,0},{2,3},{3,2},{4,5},{5,4},{6,7},{7,6},{8,9},{9,8},{10,11... | collective-permute-start | bytes 196616 | tf_op jit(solution)/shard_map/ppermute | solution.py:44
  8.4 4.7 %collective-permute-start.2 = (s32[8,128]{1,0:T(8,128)S(1)}, s32[8,128]{1,0:T(8,128)S(1)}, u32[]{:S(2)}, u32[]{:S(2)}) collective-permute-start(s32[8,128]{1,0:T(8,128)S(1)} %get-tuple-element.8.maps), channel_id=1, source_target_pairs={{0,8},{1,17},{2,10},{3,19},{4,12},{5,21},{6,14},{7,23},{8,0},{9,25... | collective-permute-start | bytes 12296 | tf_op jit(solution)/shard_map/ppermute | solution.py:44
  9.2 7.9 %collective-permute-start.5 = (f32[128,256]{1,0:T(8,128)S(1)}, f32[128,256]{1,0:T(8,128)S(1)}, u32[]{:S(2)}, u32[]{:S(2)}) collective-permute-start(f32[128,256]{1,0:T(8,128)S(1)} %pair.1.after.refs_0_), channel_id=1, source_target_pairs={{0,4},{1,7},{2,6},{3,5},{4,0},{5,3},{6,2},{7,1},{8,12},{9,15},{10,... | collective-permute-start | bytes 393224 | tf_op jit(solution)/shard_map/ppermute | solution.py:44
  11.8 6.3 %collective-permute-start.4 = (f32[128,256]{1,0:T(8,128)S(1)}, f32[128,256]{1,0:T(8,128)S(1)}, u32[]{:S(2)}, u32[]{:S(2)}) collective-permute-start(f32[128,256]{1,0:T(8,128)S(1)} %get-tuple-element.9), channel_id=1, source_target_pairs={{0,8},{1,17},{2,10},{3,19},{4,12},{5,21},{6,14},{7,23},{8,0},{9,25... | collective-permute-start | bytes 393224 | tf_op jit(solution)/shard_map/ppermute | solution.py:44
  13.9 9.4 %collective-permute-start.8 = (f32[8,128,128]{2,1,0:T(8,128)S(1)}, f32[8,128,128]{2,1,0:T(8,128)S(1)}, u32[]{:S(2)}, u32[]{:S(2)}) collective-permute-start(f32[8,128,128]{2,1,0:T(8,128)S(1)} %send.1.after), channel_id=1, source_target_pairs={{0,16},{1,9},{2,18},{3,11},{4,20},{5,13},{6,22},{7,15},{8,24},{9,1... | collective-permute-start | bytes 1572872 | tf_op jit(solution)/shard_map/ppermute | solution.py:44
  15.5 4.3 %collective-permute-start.6 = (f32[64,256]{1,0:T(8,128)S(1)}, f32[64,256]{1,0:T(8,128)S(1)}, u32[]{:S(2)}, u32[]{:S(2)}) collective-permute-start(f32[64,256]{1,0:T(8,128)S(1)} %copy-done), channel_id=1, source_target_pairs={{0,2},{1,3},{2,0},{3,1},{4,6},{5,7},{6,4},{7,5},{8,10},{9,11},{10,... | collective-permute-start | bytes 196616 | tf_op jit(solution)/shard_map/ppermute | solution.py:44
  19.8 1.5 %collective-permute-start.7 = (f32[192,256]{1,0:T(8,128)S(1)}, f32[192,256]{1,0:T(8,128)S(1)}, u32[]{:S(2)}, u32[]{:S(2)}) collective-permute-start(f32[192,256]{1,0:T(8,128)S(1)} %merge.1.refs_3_), channel_id=1, source_target_pairs={{0,1},{1,0},{2,3},{3,2},{4,5},{5,4},{6,7},{7,6},{8,9},{9,8},{10,11... | collective-permute-start | bytes 589832 | tf_op jit(solution)/shard_map/ppermute | solution.py:44

commit v3 on v2

--- a/solution.py
+++ b/solution.py
@@ -14,7 +14,7 @@
 LINES, LANES = 8, 128
 LOW, OWN, OUT, OTHER = 0, 1, 2, 3
 f32, i32 = jnp.float32, jnp.int32
-COST = dict(hint=1 << 33, label=0, pack=0, pair=0, send=1 << 30, merge=0, part=1 << 31, last=0)
+COST = dict(hint=1 << 33, label=0, pair=0, pack=0, send=1 << 30, mark=34 << 25, merge=0, part=0, last=0)
 
 
 class Plan:
@@ -67,45 +67,51 @@
     mark[...] = jnp.zeros_like(mark)
 
 
-def label_kernel(n, mark, panel, low, own, out, labelled):
-    labelled[0:n] = panel[...]
-    labelled[n:] = jnp.zeros((LINES, labelled.shape[1]), f32)
+def label_kernel(mark, low, own, out, maps):
+    maps[...] = jnp.zeros_like(maps)
     for line, ref in ((LOW, low), (OWN, own), (OUT, out)):
-        labelled[n + line : n + line + 1, 0 : ref.shape[2]] = ref[0].astype(f32)
-
-
-def pair_kernel(n, mark, own, other, joined):
+        maps[line : line + 1, 0 : ref.shape[2]] = ref[0]
+
+
+def pair_kernel(n, after, own, other, joined):
     joined[0:n] = own[...]
     joined[n : 2 * n] = other[...]
 
 
-def pack_kernel(n, after, labelled, other, panels, maps):
-    panels[0:n] = labelled[0:n]
-    panels[n : 2 * n] = other[0:n]
+def pack_kernel(after, own, other, maps):
     maps[...] = jnp.zeros_like(maps)
-    maps[0:3] = labelled[n : n + 3, 0:LANES].astype(i32)
-    maps[3:6] = other[n : n + 3, 0:LANES].astype(i32)
-
-
-def merge_kernel(n, after, also, along, next_to, joined):
-    joined[0 : 2 * n] = along[...]
-    joined[2 * n : 3 * n] = next_to[...]
+    maps[0:OTHER] = own[0:OTHER]
+    maps[OTHER : 2 * OTHER] = other[0:OTHER]
+
+
+def merge_kernel(n, after, near, far, along, joined):
+    for k, ref in enumerate((along, near, far)):
+        joined[2 * n * k : 2 * n * (k + 1)] = ref[...]
+
+
+def mark_kernel(after, along, mark):
+    mark[...] = along[0:LINES, 0:LANES]
+
+
+def scalars(values, count):
+    return [values[0, u] for u in range(count)]
 
 
 def send_kernel(plan, maps, maps_met, mine, met, sent):
-    if not plan.balanced:
+    line = lambda ref, k: jnp.broadcast_to(ref[k : k + 1, :], (LINES, LANES))
+    through = lambda targets, slots: jnp.take_along_axis(targets, slots, axis=1, mode="promise_in_bounds")
+    if plan.balanced:
+        odd = plan.is_odd()
+        own_slots = jnp.where(odd, through(line(maps, OTHER + OWN), line(maps, LOW)), line(maps, OUT))
+        target = jnp.where(odd, line(maps_met, OTHER + OUT), line(maps, OUT))
+        met_slots = through(target, line(maps_met, LOW))
+        sent[...] = jnp.zeros_like(sent)
+        for u, slot in enumerate(scalars(own_slots, plan.slots)):
+            sent[slot] += mine[0, 0, u]
+    else:
+        met_slots = line(maps_met, LOW)
         sent[...] = mine[0, 0]
-        for u in range(plan.slots):
-            sent[maps_met[LOW, u]] += met[0, 0, u]
-        return
-    odd = plan.is_odd()
-    sent[...] = jnp.zeros_like(sent)
-    for u in range(plan.slots):
-        slot = jnp.where(odd, maps[OTHER + OWN, maps[LOW, u]], maps[OUT, u])
-        sent[slot] += mine[0, 0, u]
-    for u in range(plan.slots):
-        slot = maps_met[LOW, u]
-        slot = jnp.where(odd, maps_met[OTHER + OUT, slot], maps[OUT, slot])
+    for u, slot in enumerate(scalars(met_slots, plan.slots)):
         sent[slot] += met[0, 0, u]
 
 
@@ -174,7 +180,7 @@
     return call(
         functools.partial(send_kernel, plan),
         jax.ShapeDtypeStruct(updates.shape[2:], f32),
-        [SMEM] * len(maps) + [VMEM] * 2,
+        [VMEM] * (len(maps) + 2),
         (*maps, updates, met),
         "send",
     )
@@ -211,6 +217,7 @@
 def any_mesh(plan, updates, pivot_panel, map_low, map_own, map_out):
     met = plan.swap(updates, 0)
     own_maps = jnp.concatenate([map_low[0], map_own[0], map_out[0]])
+    own_maps = jnp.pad(own_maps, ((0, 0), (0, LANES - plan.slots)))
     maps = jnp.concatenate([own_maps, plan.swap(own_maps, 1)])
     maps_met = plan.swap(maps, 0)
     got = plan.swap(add_sent(plan, [maps, maps_met], updates, met), 1)
@@ -228,55 +235,46 @@
 def four_by_eight(plan, updates, pivot_panel, map_low, map_own, map_out):
     n, depth = plan.part_rows, plan.depth
     shape = jax.ShapeDtypeStruct
-    sibling = plan.move(pivot_panel, (0, 1), (0, 1))
     met = plan.swap(updates, 0)
     mark = call(hint_kernel, shape((LINES, LANES), f32), [], (), "hint")
-    labelled = call(
-        functools.partial(label_kernel, n),
-        shape((n + LINES, depth), f32),
-        [VMEM] * 5,
-        (mark, pivot_panel, map_low, map_own, map_out),
-        "label",
-    )
-    other = plan.swap(labelled, 1)
+    (panel_late,) = after(mark, pivot_panel)
+    sibling = plan.move(panel_late, (0, 1), (0, 1))
+    lines = shape((LINES, LANES), i32)
+    own_maps = call(label_kernel, lines, [VMEM] * 4, (mark, map_low, map_own, map_out), "label")
+    other_maps = plan.swap(own_maps, 1)
     pair = call(
         functools.partial(pair_kernel, n),
         shape((2 * n, depth), f32),
         [VMEM] * 3,
-        (labelled, pivot_panel, sibling),
+        (own_maps, pivot_panel, sibling),
         "pair",
     )
     along = plan.move(pair, (0, 4), (0, 6))
-    panels, maps = call(
-        functools.partial(pack_kernel, n),
-        [shape((2 * n, depth), f32), shape((LINES, LANES), i32)],
-        [VMEM] * 3,
-        (pair, labelled, other),
-        "pack",
-    )
+    maps = call(pack_kernel, lines, [VMEM] * 3, (pair, own_maps, other_maps), "pack")
     maps_met = plan.swap(maps, 0)
-    panels_met = plan.swap(panels, 0)
+    (pair_late,) = after(maps, pair)
+    x, y = plan.low, plan.up
+    near = plan.move(pair_late, (x, 0), (y, 0))
+    far = plan.move(pair_late, (x ^ y, 0), (0, 2))
 
     sent = add_sent(plan, [maps, maps_met], updates, met)
     got = plan.swap(sent, 1)
 
-    (panel_late,) = after(sent, pivot_panel)
-    next_to = plan.move(panel_late, (0, 2), (0, 2))
+    mark = call(mark_kernel, shape((LINES, LANES), f32), [VMEM] * 2, (sent, along), "mark")
+    far, near, mark = lax.optimization_barrier((far, near, mark))
     merged = call(
         functools.partial(merge_kernel, n),
-        shape((3 * n, depth), f32),
+        shape((6 * n, depth), f32),
         [VMEM] * 4,
-        (sent, panels_met, along, next_to),
+        (mark, near, far, along),
         "merge",
     )
     shared = plan.move(merged, (0, 1), (0, 1))
-    (s0, s1), (o0, o1) = ((plan.offset(0, k), plan.offset(1, k)) for k in range(2))
+    own = [[(ROW, 0), (COL, 0)], [(COL, 1)]]
     cols = lambda b: [[(COL, b)], [(COL, b ^ 1)]]
-    rows = lambda s, o: [[[(ROW, o)]], [[(ROW, s)], [(ROW, s ^ o)]]]
-    own = [[(ROW, 0), (COL, 0)], [(COL, 1)]]
-    even = [own, *rows(s0, o0), cols(4) + [[(COL, 2)]], cols(7) + [[(COL, 3)]]]
-    odd = [own, *rows(s1, o1), cols(6) + [[(COL, 2)]], cols(5) + [[(COL, 3)]]]
-    panels = [pair, other, panels_met, merged, shared]
+    even = [own, cols(4) + [[(ROW, x)], [], [(ROW, x ^ y)], []], cols(7) + [[], [(ROW, y)]] + cols(3)]
+    odd = [own, cols(6) + [[(ROW, y)], []] + cols(2), cols(5) + [[], [(ROW, x)], [], [(ROW, x ^ y)]]]
+    panels = [pair, merged, shared]
     part = add_part(plan, (even, odd), (maps, maps_met), updates, met, panels)
     return add_last(plan, [], part, got)
 

time: 24.3 us -> 22 us (0.905)
  waiting for transfers between devices: 7.79 us -> 6.18 us
  Pallas kernels: 3.76 us -> 3.23 us
    ppermute x9, waiting for transfers between devices: 7.79 us -> 6.18 us  [move(): return lax.ppermute(shard, AXES, pairs)]
    pallas_call x8 -> x9, Pallas kernels: 3.76 us -> 3.23 us  [call(): pl.pallas_call(kernel, out_shape=outs, in_specs=in_specs, out_specs=[VMEM...]
where the time goes in v3:
time: 22 us; the launch traced here: 21.9 us
  starting transfers between devices  12.4 us (56%)
  waiting for transfers between devices  6.18 us (28%)
  Pallas kernels  3.23 us (15%)
    ppermute x9, starting transfers between devices, move(): return lax.ppermute(shard, AXES, pairs)  12.4 us
    ppermute x9, waiting for transfers between devices, move(): return lax.ppermute(shard, AXES, pairs)  6.18 us
    pallas_call x9, Pallas kernels, call(): pl.pallas_call(kernel, out_shape=outs, in_specs=in_specs, out_specs=[VMEM...  3.23 us
  transfers between devices with their start and end apart: 9, of which 5 were waited for; matrix products, arithmetic and copies ran while one was open for 0% of the time, Pallas kernels for 9%

profile of v3, /device:TPU:0, one launch (start us, length us, event | category | flops | bytes accessed | tf_op | source)
XLA Modules:
  0.0 21.9 jit_solution(478469827005449605)
XLA Ops:
  0.0 0.0 copy-start
  0.0 0.0 copy-start.1
  0.0 0.0 copy-start.4
  0.0 0.0 copy-start.3
  0.0 0.0 copy-start.2
  0.0 3.0 %collective-permute-start.3 = (f32[1,1,8,128,128]{4,3,2,1,0:T(8,128)}, f32[1,1,8,128,128]{4,3,2,1,0:T(8,128)S(1)}, u32[]{:S(2)}, u32[]{:S(2)}) collective-permute-start(f32[1,1,8,128,128]{4,3,2,1,0:T(8,128)} %mine.3), channel_id=1, source_target_pairs={{0,8},{1,17},{2,10},{3,19},{4,12},{5,21},{6,14},{7,23},{8,0},{9,25... | collective-permute-start | bytes 1572872 | tf_op jit(solution)/shard_map/ppermute | solution.py:44
  3.0 0.0 copy-done.1
  3.0 0.0 collective-permute-start
  3.0 0.0 copy-done.4
  3.0 0.0 copy-done.3
  3.1 0.0 copy-done.2
  3.1 1.6 %collective-permute-start.1 = (s32[8,128]{1,0:T(8,128)S(1)}, s32[8,128]{1,0:T(8,128)S(1)}, u32[]{:S(2)}, u32[]{:S(2)}) collective-permute-start(s32[8,128]{1,0:T(8,128)S(1)} %label.1.after.own), channel_id=1, source_target_pairs={{0,16},{1,9},{2,18},{3,11},{4,20},{5,13},{6,22},{7,15},{8,24},{9,1... | collective-permute-start | bytes 12296 | tf_op jit(solution)/shard_map/ppermute | solution.py:44
  4.7 0.0 collective-permute-done.other
  4.7 2.7 %collective-permute-start.6 = (f32[128,256]{1,0:T(8,128)S(1)}, f32[128,256]{1,0:T(8,128)S(1)}, u32[]{:S(2)}, u32[]{:S(2)}) collective-permute-start(f32[128,256]{1,0:T(8,128)S(1)} %pair.1.after.refs_0_), channel_id=1, source_target_pairs={{0,4},{1,7},{2,6},{3,5},{4,0},{5,3},{6,2},{7,1},{8,12},{9,15},{10,... | collective-permute-start | bytes 393224 | tf_op jit(solution)/shard_map/ppermute | solution.py:44
  7.3 0.0 collective-permute-done.1.other
  7.3 0.8 %collective-permute-start.2 = (s32[8,128]{1,0:T(8,128)S(1)}, s32[8,128]{1,0:T(8,128)S(1)}, u32[]{:S(2)}, u32[]{:S(2)}) collective-permute-start(s32[8,128]{1,0:T(8,128)S(1)} %pack.1.maps), channel_id=1, source_target_pairs={{0,8},{1,17},{2,10},{3,19},{4,12},{5,21},{6,14},{7,23},{8,0},{9,25... | collective-permute-start | bytes 12296 | tf_op jit(solution)/shard_map/ppermute | solution.py:44
  8.1 1.2 %collective-permute-start.5 = (f32[128,256]{1,0:T(8,128)S(1)}, f32[128,256]{1,0:T(8,128)S(1)}, u32[]{:S(2)}, u32[]{:S(2)}) collective-permute-start(f32[128,256]{1,0:T(8,128)S(1)} %pair.1.after.refs_0_), channel_id=1, source_target_pairs={{0,8},{1,17},{2,10},{3,19},{4,12},{5,21},{6,14},{7,23},{8,0},{9,25... | collective-permute-start | bytes 393224 | tf_op jit(solution)/shard_map/ppermute | solution.py:44
  9.4 1.4 %collective-permute-start.4 = (f32[128,256]{1,0:T(8,128)S(1)}, f32[128,256]{1,0:T(8,128)S(1)}, u32[]{:S(2)}, u32[]{:S(2)}) collective-permute-start(f32[128,256]{1,0:T(8,128)S(1)} %pair.1.after.refs_0_), channel_id=1, source_target_pairs={{0,24},{1,3},{2,26},{3,1},{4,28},{5,7},{6,30},{7,5},{8,16},{9,11},... | collective-permute-start | bytes 393224 | tf_op jit(solution)/shard_map/ppermute | solution.py:44
  10.8 0.2 collective-permute-done.2.maps_met
  11.0 0.0 collective-permute-done.3.met
  11.0 0.0 copy-done
  11.0 0.3 %send.1.after = f32[8,128,128]{2,1,0:T(8,128)S(1)} custom-call(s32[8,128]{1,0:T(8,128)S(1)} %pack.1.maps, s32[8,128]{1,0:T(8,128)S(1)} %collective-permute-done.2.maps_met, f32[1,1,8,128,128]{4,3,2,1,0:T(8,128)S(1)} %copy-done, f32[1,1,8,128,128]{4,3,2,1,0:T(8,128)S(1)} %collective-permute-done.3.met), custom_call_target="tpu_custom_call" | custom-call | flops 1073741824 | tf_op jit(solution)/shard_map/send/pallas_call | solution.py:54
  11.3 1.7 %collective-permute-start.8 = (f32[8,128,128]{2,1,0:T(8,128)S(1)}, f32[8,128,128]{2,1,0:T(8,128)S(1)}, u32[]{:S(2)}, u32[]{:S(2)}) collective-permute-start(f32[8,128,128]{2,1,0:T(8,128)S(1)} %send.1.after), channel_id=1, source_target_pairs={{0,16},{1,9},{2,18},{3,11},{4,20},{5,13},{6,22},{7,15},{8,24},{9,1... | collective-permute-start | bytes 1572872 | tf_op jit(solution)/shard_map/ppermute | solution.py:44
  12.9 0.9 %collective-permute-done.6.along = f32[128,256]{1,0:T(8,128)S(1)} collective-permute-done((f32[128,256]{1,0:T(8,128)S(1)}, f32[128,256]{1,0:T(8,128)S(1)}, u32[]{:S(2)}, u32[]{:S(2)}) %collective-permute-start.6) | collective-permute-done | bytes 131104 | tf_op jit(solution)/shard_map/ppermute | solution.py:44
  13.9 0.0 collective-permute-done.5.near
  13.9 2.1 %collective-permute-done.4.far = f32[128,256]{1,0:T(8,128)S(1)} collective-permute-done((f32[128,256]{1,0:T(8,128)S(1)}, f32[128,256]{1,0:T(8,128)S(1)}, u32[]{:S(2)}, u32[]{:S(2)}) %collective-permute-start.4) | collective-permute-done | bytes 131104 | tf_op jit(solution)/shard_map/ppermute | solution.py:44
  16.0 0.1 collective-permute-start.7
  16.1 1.7 %collective-permute-done.7.refs_2_ = f32[384,256]{1,0:T(8,128)S(1)} collective-permute-done((f32[384,256]{1,0:T(8,128)S(1)}, f32[384,256]{1,0:T(8,128)S(1)}, u32[]{:S(2)}, u32[]{:S(2)}) %collective-permute-start.7) | collective-permute-done | bytes 393248 | tf_op jit(solution)/shard_map/ppermute | solution.py:44
  17.8 2.0 %part.1.refs_0_ = f32[256,512]{1,0:T(8,128)S(1)} custom-call(s32[8,128]{1,0:T(8,128)S(1)} %pack.1.maps, s32[8,128]{1,0:T(8,128)S(1)} %collective-permute-done.2.maps_met, f32[1,1,8,128,128]{4,3,2,1,0:T(8,128)S(1)} %copy-done, f32[1,1,8,128,128]{4,3,2,1,0:T(8,128)S(1)} %collective-permute-done.3.met, f32[128,256]{1,0:T(8,128)S(1)} %pair.1.after.refs_0_, ...), custom_call_target="tpu_custom_call" | custom-call | tf_op jit(solution)/shard_map/part/pallas_call | solution.py:54
  19.8 1.2 %collective-permute-done.8.refs_1_ = f32[8,128,128]{2,1,0:T(8,128)S(1)} collective-permute-done((f32[8,128,128]{2,1,0:T(8,128)S(1)}, f32[8,128,128]{2,1,0:T(8,128)S(1)}, u32[]{:S(2)}, u32[]{:S(2)}) %collective-permute-start.8) | collective-permute-done | bytes 524320 | tf_op jit(solution)/shard_map/ppermute | solution.py:44
  21.1 0.8 %last.1 = f32[256,512]{1,0:T(8,128)} custom-call(f32[256,512]{1,0:T(8,128)S(1)} %part.1.refs_0_, f32[8,128,128]{2,1,0:T(8,128)S(1)} %collective-permute-done.8.refs_1_), custom_call_target="tpu_custom_call" | custom-call | tf_op jit(solution)/shard_map/last/pallas_call | solution.py:54
  (6 shorter events, 0.0 us)
Async XLA Ops:
  0.0 11.0 %copy-start = (f32[1,1,8,128,128]{4,3,2,1,0:T(8,128)S(1)}, f32[1,1,8,128,128]{4,3,2,1,0:T(8,128)}, u32[]{:S(2)}) copy-start(f32[1,1,8,128,128]{4,3,2,1,0:T(8,128)} %mine.3) | copy-start | bytes 1572868
  0.0 3.0 %copy-start.1 = (f32[64,256]{1,0:T(8,128)S(1)}, f32[64,256]{1,0:T(8,128)}, u32[]{:S(2)}) copy-start(f32[64,256]{1,0:T(8,128)} %own.3) | copy-start | bytes 196612
  0.0 3.0 %copy-start.4 = (s32[1,1,8]{2,1,0:T(1,128)S(1)}, s32[1,1,8]{2,1,0:T(1,128)}, u32[]{:S(2)}) copy-start(s32[1,1,8]{2,1,0:T(1,128)} %out.1) | copy-start | bytes 100
  0.0 3.0 %copy-start.3 = (s32[1,1,8]{2,1,0:T(1,128)S(1)}, s32[1,1,8]{2,1,0:T(1,128)}, u32[]{:S(2)}) copy-start(s32[1,1,8]{2,1,0:T(1,128)} %own.2) | copy-start | bytes 100
  0.0 3.0 %copy-start.2 = (s32[1,1,8]{2,1,0:T(1,128)S(1)}, s32[1,1,8]{2,1,0:T(1,128)}, u32[]{:S(2)}) copy-start(s32[1,1,8]{2,1,0:T(1,128)} %low.1) | copy-start | bytes 100
  0.0 10.9 %collective-permute-start.3 = (f32[1,1,8,128,128]{4,3,2,1,0:T(8,128)}, f32[1,1,8,128,128]{4,3,2,1,0:T(8,128)S(1)}, u32[]{:S(2)}, u32[]{:S(2)}) collective-permute-start(f32[1,1,8,128,128]{4,3,2,1,0:T(8,128)} %mine.3), channel_id=1, source_target_pairs={{0,8},{1,17},{2,10},{3,19},{4,12},{5,21},{6,14},{7,23},{8,0},{9,25... | collective-permute-start | bytes 1572872 | tf_op jit(solution)/shard_map/ppermute | solution.py:44
  3.0 1.6 %collective-permute-start = (f32[64,256]{1,0:T(8,128)S(1)}, f32[64,256]{1,0:T(8,128)S(1)}, u32[]{:S(2)}, u32[]{:S(2)}) collective-permute-start(f32[64,256]{1,0:T(8,128)S(1)} %copy-done.1), channel_id=1, source_target_pairs={{0,1},{1,0},{2,3},{3,2},{4,5},{5,4},{6,7},{7,6},{8,9},{9,8},{10,11... | collective-permute-start | bytes 196616 | tf_op jit(solution)/shard_map/ppermute | solution.py:44
  3.1 4.3 %collective-permute-start.1 = (s32[8,128]{1,0:T(8,128)S(1)}, s32[8,128]{1,0:T(8,128)S(1)}, u32[]{:S(2)}, u32[]{:S(2)}) collective-permute-start(s32[8,128]{1,0:T(8,128)S(1)} %label.1.after.own), channel_id=1, source_target_pairs={{0,16},{1,9},{2,18},{3,11},{4,20},{5,13},{6,22},{7,15},{8,24},{9,1... | collective-permute-start | bytes 12296 | tf_op jit(solution)/shard_map/ppermute | solution.py:44
  4.7 9.2 %collective-permute-start.6 = (f32[128,256]{1,0:T(8,128)S(1)}, f32[128,256]{1,0:T(8,128)S(1)}, u32[]{:S(2)}, u32[]{:S(2)}) collective-permute-start(f32[128,256]{1,0:T(8,128)S(1)} %pair.1.after.refs_0_), channel_id=1, source_target_pairs={{0,4},{1,7},{2,6},{3,5},{4,0},{5,3},{6,2},{7,1},{8,12},{9,15},{10,... | collective-permute-start | bytes 393224 | tf_op jit(solution)/shard_map/ppermute | solution.py:44
  7.3 3.6 %collective-permute-start.2 = (s32[8,128]{1,0:T(8,128)S(1)}, s32[8,128]{1,0:T(8,128)S(1)}, u32[]{:S(2)}, u32[]{:S(2)}) collective-permute-start(s32[8,128]{1,0:T(8,128)S(1)} %pack.1.maps), channel_id=1, source_target_pairs={{0,8},{1,17},{2,10},{3,19},{4,12},{5,21},{6,14},{7,23},{8,0},{9,25... | collective-permute-start | bytes 12296 | tf_op jit(solution)/shard_map/ppermute | solution.py:44
  8.1 5.7 %collective-permute-start.5 = (f32[128,256]{1,0:T(8,128)S(1)}, f32[128,256]{1,0:T(8,128)S(1)}, u32[]{:S(2)}, u32[]{:S(2)}) collective-permute-start(f32[128,256]{1,0:T(8,128)S(1)} %pair.1.after.refs_0_), channel_id=1, source_target_pairs={{0,8},{1,17},{2,10},{3,19},{4,12},{5,21},{6,14},{7,23},{8,0},{9,25... | collective-permute-start | bytes 393224 | tf_op jit(solution)/shard_map/ppermute | solution.py:44
  9.4 6.6 %collective-permute-start.4 = (f32[128,256]{1,0:T(8,128)S(1)}, f32[128,256]{1,0:T(8,128)S(1)}, u32[]{:S(2)}, u32[]{:S(2)}) collective-permute-start(f32[128,256]{1,0:T(8,128)S(1)} %pair.1.after.refs_0_), channel_id=1, source_target_pairs={{0,24},{1,3},{2,26},{3,1},{4,28},{5,7},{6,30},{7,5},{8,16},{9,11},... | collective-permute-start | bytes 393224 | tf_op jit(solution)/shard_map/ppermute | solution.py:44
  11.3 9.8 %collective-permute-start.8 = (f32[8,128,128]{2,1,0:T(8,128)S(1)}, f32[8,128,128]{2,1,0:T(8,128)S(1)}, u32[]{:S(2)}, u32[]{:S(2)}) collective-permute-start(f32[8,128,128]{2,1,0:T(8,128)S(1)} %send.1.after), channel_id=1, source_target_pairs={{0,16},{1,9},{2,18},{3,11},{4,20},{5,13},{6,22},{7,15},{8,24},{9,1... | collective-permute-start | bytes 1572872 | tf_op jit(solution)/shard_map/ppermute | solution.py:44
  16.0 1.8 %collective-permute-start.7 = (f32[384,256]{1,0:T(8,128)S(1)}, f32[384,256]{1,0:T(8,128)S(1)}, u32[]{:S(2)}, u32[]{:S(2)}) collective-permute-start(f32[384,256]{1,0:T(8,128)S(1)} %merge.1.refs_1_), channel_id=1, source_target_pairs={{0,1},{1,0},{2,3},{3,2},{4,5},{5,4},{6,7},{7,6},{8,9},{9,8},{10,11... | collective-permute-start | bytes 1179656 | tf_op jit(solution)/shard_map/ppermute | solution.py:44

commit v4 on v3

--- a/solution.py
+++ b/solution.py
@@ -255,7 +255,7 @@
     (pair_late,) = after(maps, pair)
     x, y = plan.low, plan.up
     near = plan.move(pair_late, (x, 0), (y, 0))
-    far = plan.move(pair_late, (x ^ y, 0), (0, 2))
+    far = plan.move(pair_late, (0, 2), (x ^ y, 0))
 
     sent = add_sent(plan, [maps, maps_met], updates, met)
     got = plan.swap(sent, 1)
@@ -272,8 +272,8 @@
     shared = plan.move(merged, (0, 1), (0, 1))
     own = [[(ROW, 0), (COL, 0)], [(COL, 1)]]
     cols = lambda b: [[(COL, b)], [(COL, b ^ 1)]]
-    even = [own, cols(4) + [[(ROW, x)], [], [(ROW, x ^ y)], []], cols(7) + [[], [(ROW, y)]] + cols(3)]
-    odd = [own, cols(6) + [[(ROW, y)], []] + cols(2), cols(5) + [[], [(ROW, x)], [], [(ROW, x ^ y)]]]
+    even = [own, cols(4) + [[(ROW, x)], []] + cols(2), cols(7) + [[], [(ROW, y)], [], [(ROW, x ^ y)]]]
+    odd = [own, cols(6) + [[(ROW, y)], [], [(ROW, x ^ y)], []], cols(5) + [[], [(ROW, x)]] + cols(3)]
     panels = [pair, merged, shared]
     part = add_part(plan, (even, odd), (maps, maps_met), updates, met, panels)
     return add_last(plan, [], part, got)

time: 22 us -> 21.7 us (0.986)
  waiting for transfers between devices: 6.18 us -> 5.66 us
    ppermute x9, waiting for transfers between devices: 6.18 us -> 5.66 us  [move(): return lax.ppermute(shard, AXES, pairs)]
  transfers between devices with their start and end apart: 9 -> 9, of which waited for: 5 -> 4; matrix products, arithmetic and copies ran while one was open for 0% -> 0% of each run, Pallas kernels for 9% -> 10%
where the time goes in v4:
time: 21.7 us; the launch traced here: 21.6 us
  starting transfers between devices  12.6 us (58%)
  waiting for transfers between devices  5.66 us (26%)
  Pallas kernels  3.23 us (15%)
    ppermute x9, starting transfers between devices, move(): return lax.ppermute(shard, AXES, pairs)  12.6 us
    ppermute x9, waiting for transfers between devices, move(): return lax.ppermute(shard, AXES, pairs)  5.66 us
    pallas_call x9, Pallas kernels, call(): pl.pallas_call(kernel, out_shape=outs, in_specs=in_specs, out_specs=[VMEM...  3.23 us
  transfers between devices with their start and end apart: 9, of which 4 were waited for; matrix products, arithmetic and copies ran while one was open for 0% of the time, Pallas kernels for 10%

profile of v4, /device:TPU:0, one launch (start us, length us, event | category | flops | bytes accessed | tf_op | source)
XLA Modules:
  0.0 21.6 jit_solution(8802077922567039813)
XLA Ops:
  0.0 0.0 copy-start
  0.0 0.0 copy-start.1
  0.0 0.0 copy-start.4
  0.0 0.0 copy-start.3
  0.0 0.0 copy-start.2
  0.0 3.0 %collective-permute-start.3 = (f32[1,1,8,128,128]{4,3,2,1,0:T(8,128)}, f32[1,1,8,128,128]{4,3,2,1,0:T(8,128)S(1)}, u32[]{:S(2)}, u32[]{:S(2)}) collective-permute-start(f32[1,1,8,128,128]{4,3,2,1,0:T(8,128)} %mine.3), channel_id=1, source_target_pairs={{0,8},{1,17},{2,10},{3,19},{4,12},{5,21},{6,14},{7,23},{8,0},{9,25... | collective-permute-start | bytes 1572872 | tf_op jit(solution)/shard_map/ppermute | solution.py:44
  3.0 0.0 copy-done.1
  3.0 0.0 collective-permute-start
  3.0 0.0 copy-done.4
  3.0 0.0 copy-done.3
  3.1 0.0 copy-done.2
  3.1 1.6 %collective-permute-start.1 = (s32[8,128]{1,0:T(8,128)S(1)}, s32[8,128]{1,0:T(8,128)S(1)}, u32[]{:S(2)}, u32[]{:S(2)}) collective-permute-start(s32[8,128]{1,0:T(8,128)S(1)} %label.1.after.own), channel_id=1, source_target_pairs={{0,16},{1,9},{2,18},{3,11},{4,20},{5,13},{6,22},{7,15},{8,24},{9,1... | collective-permute-start | bytes 12296 | tf_op jit(solution)/shard_map/ppermute | solution.py:44
  4.7 0.0 collective-permute-done.other
  4.7 2.7 %collective-permute-start.6 = (f32[128,256]{1,0:T(8,128)S(1)}, f32[128,256]{1,0:T(8,128)S(1)}, u32[]{:S(2)}, u32[]{:S(2)}) collective-permute-start(f32[128,256]{1,0:T(8,128)S(1)} %pair.1.after.refs_0_), channel_id=1, source_target_pairs={{0,4},{1,7},{2,6},{3,5},{4,0},{5,3},{6,2},{7,1},{8,12},{9,15},{10,... | collective-permute-start | bytes 393224 | tf_op jit(solution)/shard_map/ppermute | solution.py:44
  7.3 0.0 collective-permute-done.1.other
  7.3 0.8 %collective-permute-start.2 = (s32[8,128]{1,0:T(8,128)S(1)}, s32[8,128]{1,0:T(8,128)S(1)}, u32[]{:S(2)}, u32[]{:S(2)}) collective-permute-start(s32[8,128]{1,0:T(8,128)S(1)} %pack.1.maps), channel_id=1, source_target_pairs={{0,8},{1,17},{2,10},{3,19},{4,12},{5,21},{6,14},{7,23},{8,0},{9,25... | collective-permute-start | bytes 12296 | tf_op jit(solution)/shard_map/ppermute | solution.py:44
  8.1 1.2 %collective-permute-start.5 = (f32[128,256]{1,0:T(8,128)S(1)}, f32[128,256]{1,0:T(8,128)S(1)}, u32[]{:S(2)}, u32[]{:S(2)}) collective-permute-start(f32[128,256]{1,0:T(8,128)S(1)} %pair.1.after.refs_0_), channel_id=1, source_target_pairs={{0,8},{1,17},{2,10},{3,19},{4,12},{5,21},{6,14},{7,23},{8,0},{9,25... | collective-permute-start | bytes 393224 | tf_op jit(solution)/shard_map/ppermute | solution.py:44
  9.4 1.6 %collective-permute-start.4 = (f32[128,256]{1,0:T(8,128)S(1)}, f32[128,256]{1,0:T(8,128)S(1)}, u32[]{:S(2)}, u32[]{:S(2)}) collective-permute-start(f32[128,256]{1,0:T(8,128)S(1)} %pair.1.after.refs_0_), channel_id=1, source_target_pairs={{0,2},{1,25},{2,0},{3,27},{4,6},{5,29},{6,4},{7,31},{8,10},{9,17},... | collective-permute-start | bytes 393224 | tf_op jit(solution)/shard_map/ppermute | solution.py:44
  10.9 0.0 collective-permute-done.2.maps_met
  11.0 0.0 collective-permute-done.3.met
  11.0 0.0 copy-done
  11.0 0.3 %send.1.after = f32[8,128,128]{2,1,0:T(8,128)S(1)} custom-call(s32[8,128]{1,0:T(8,128)S(1)} %pack.1.maps, s32[8,128]{1,0:T(8,128)S(1)} %collective-permute-done.2.maps_met, f32[1,1,8,128,128]{4,3,2,1,0:T(8,128)S(1)} %copy-done, f32[1,1,8,128,128]{4,3,2,1,0:T(8,128)S(1)} %collective-permute-done.3.met), custom_call_target="tpu_custom_call" | custom-call | flops 1073741824 | tf_op jit(solution)/shard_map/send/pallas_call | solution.py:54
  11.3 1.7 %collective-permute-start.8 = (f32[8,128,128]{2,1,0:T(8,128)S(1)}, f32[8,128,128]{2,1,0:T(8,128)S(1)}, u32[]{:S(2)}, u32[]{:S(2)}) collective-permute-start(f32[8,128,128]{2,1,0:T(8,128)S(1)} %send.1.after), channel_id=1, source_target_pairs={{0,16},{1,9},{2,18},{3,11},{4,20},{5,13},{6,22},{7,15},{8,24},{9,1... | collective-permute-start | bytes 1572872 | tf_op jit(solution)/shard_map/ppermute | solution.py:44
  12.9 0.9 %collective-permute-done.6.along = f32[128,256]{1,0:T(8,128)S(1)} collective-permute-done((f32[128,256]{1,0:T(8,128)S(1)}, f32[128,256]{1,0:T(8,128)S(1)}, u32[]{:S(2)}, u32[]{:S(2)}) %collective-permute-start.6) | collective-permute-done | bytes 131104 | tf_op jit(solution)/shard_map/ppermute | solution.py:44
  13.8 0.0 collective-permute-done.5.near
  13.8 1.3 %collective-permute-done.4.far = f32[128,256]{1,0:T(8,128)S(1)} collective-permute-done((f32[128,256]{1,0:T(8,128)S(1)}, f32[128,256]{1,0:T(8,128)S(1)}, u32[]{:S(2)}, u32[]{:S(2)}) %collective-permute-start.4) | collective-permute-done | bytes 131104 | tf_op jit(solution)/shard_map/ppermute | solution.py:44
  15.2 0.1 collective-permute-start.7
  15.3 1.7 %collective-permute-done.7.refs_2_ = f32[384,256]{1,0:T(8,128)S(1)} collective-permute-done((f32[384,256]{1,0:T(8,128)S(1)}, f32[384,256]{1,0:T(8,128)S(1)}, u32[]{:S(2)}, u32[]{:S(2)}) %collective-permute-start.7) | collective-permute-done | bytes 393248 | tf_op jit(solution)/shard_map/ppermute | solution.py:44
  17.0 2.0 %part.1.refs_0_ = f32[256,512]{1,0:T(8,128)S(1)} custom-call(s32[8,128]{1,0:T(8,128)S(1)} %pack.1.maps, s32[8,128]{1,0:T(8,128)S(1)} %collective-permute-done.2.maps_met, f32[1,1,8,128,128]{4,3,2,1,0:T(8,128)S(1)} %copy-done, f32[1,1,8,128,128]{4,3,2,1,0:T(8,128)S(1)} %collective-permute-done.3.met, f32[128,256]{1,0:T(8,128)S(1)} %pair.1.after.refs_0_, ...), custom_call_target="tpu_custom_call" | custom-call | tf_op jit(solution)/shard_map/part/pallas_call | solution.py:54
  19.0 1.7 %collective-permute-done.8.refs_1_ = f32[8,128,128]{2,1,0:T(8,128)S(1)} collective-permute-done((f32[8,128,128]{2,1,0:T(8,128)S(1)}, f32[8,128,128]{2,1,0:T(8,128)S(1)}, u32[]{:S(2)}, u32[]{:S(2)}) %collective-permute-start.8) | collective-permute-done | bytes 524320 | tf_op jit(solution)/shard_map/ppermute | solution.py:44
  20.7 0.8 %last.1 = f32[256,512]{1,0:T(8,128)} custom-call(f32[256,512]{1,0:T(8,128)S(1)} %part.1.refs_0_, f32[8,128,128]{2,1,0:T(8,128)S(1)} %collective-permute-done.8.refs_1_), custom_call_target="tpu_custom_call" | custom-call | tf_op jit(solution)/shard_map/last/pallas_call | solution.py:54
  (6 shorter events, 0.0 us)
Async XLA Ops:
  0.0 11.0 %copy-start = (f32[1,1,8,128,128]{4,3,2,1,0:T(8,128)S(1)}, f32[1,1,8,128,128]{4,3,2,1,0:T(8,128)}, u32[]{:S(2)}) copy-start(f32[1,1,8,128,128]{4,3,2,1,0:T(8,128)} %mine.3) | copy-start | bytes 1572868
  0.0 3.0 %copy-start.1 = (f32[64,256]{1,0:T(8,128)S(1)}, f32[64,256]{1,0:T(8,128)}, u32[]{:S(2)}) copy-start(f32[64,256]{1,0:T(8,128)} %own.3) | copy-start | bytes 196612
  0.0 3.0 %copy-start.4 = (s32[1,1,8]{2,1,0:T(1,128)S(1)}, s32[1,1,8]{2,1,0:T(1,128)}, u32[]{:S(2)}) copy-start(s32[1,1,8]{2,1,0:T(1,128)} %out.1) | copy-start | bytes 100
  0.0 3.0 %copy-start.3 = (s32[1,1,8]{2,1,0:T(1,128)S(1)}, s32[1,1,8]{2,1,0:T(1,128)}, u32[]{:S(2)}) copy-start(s32[1,1,8]{2,1,0:T(1,128)} %own.2) | copy-start | bytes 100
  0.0 3.0 %copy-start.2 = (s32[1,1,8]{2,1,0:T(1,128)S(1)}, s32[1,1,8]{2,1,0:T(1,128)}, u32[]{:S(2)}) copy-start(s32[1,1,8]{2,1,0:T(1,128)} %low.1) | copy-start | bytes 100
  0.0 10.9 %collective-permute-start.3 = (f32[1,1,8,128,128]{4,3,2,1,0:T(8,128)}, f32[1,1,8,128,128]{4,3,2,1,0:T(8,128)S(1)}, u32[]{:S(2)}, u32[]{:S(2)}) collective-permute-start(f32[1,1,8,128,128]{4,3,2,1,0:T(8,128)} %mine.3), channel_id=1, source_target_pairs={{0,8},{1,17},{2,10},{3,19},{4,12},{5,21},{6,14},{7,23},{8,0},{9,25... | collective-permute-start | bytes 1572872 | tf_op jit(solution)/shard_map/ppermute | solution.py:44
  3.0 1.6 %collective-permute-start = (f32[64,256]{1,0:T(8,128)S(1)}, f32[64,256]{1,0:T(8,128)S(1)}, u32[]{:S(2)}, u32[]{:S(2)}) collective-permute-start(f32[64,256]{1,0:T(8,128)S(1)} %copy-done.1), channel_id=1, source_target_pairs={{0,1},{1,0},{2,3},{3,2},{4,5},{5,4},{6,7},{7,6},{8,9},{9,8},{10,11... | collective-permute-start | bytes 196616 | tf_op jit(solution)/shard_map/ppermute | solution.py:44
  3.1 4.3 %collective-permute-start.1 = (s32[8,128]{1,0:T(8,128)S(1)}, s32[8,128]{1,0:T(8,128)S(1)}, u32[]{:S(2)}, u32[]{:S(2)}) collective-permute-start(s32[8,128]{1,0:T(8,128)S(1)} %label.1.after.own), channel_id=1, source_target_pairs={{0,16},{1,9},{2,18},{3,11},{4,20},{5,13},{6,22},{7,15},{8,24},{9,1... | collective-permute-start | bytes 12296 | tf_op jit(solution)/shard_map/ppermute | solution.py:44
  4.7 9.2 %collective-permute-start.6 = (f32[128,256]{1,0:T(8,128)S(1)}, f32[128,256]{1,0:T(8,128)S(1)}, u32[]{:S(2)}, u32[]{:S(2)}) collective-permute-start(f32[128,256]{1,0:T(8,128)S(1)} %pair.1.after.refs_0_), channel_id=1, source_target_pairs={{0,4},{1,7},{2,6},{3,5},{4,0},{5,3},{6,2},{7,1},{8,12},{9,15},{10,... | collective-permute-start | bytes 393224 | tf_op jit(solution)/shard_map/ppermute | solution.py:44
  7.3 3.6 %collective-permute-start.2 = (s32[8,128]{1,0:T(8,128)S(1)}, s32[8,128]{1,0:T(8,128)S(1)}, u32[]{:S(2)}, u32[]{:S(2)}) collective-permute-start(s32[8,128]{1,0:T(8,128)S(1)} %pack.1.maps), channel_id=1, source_target_pairs={{0,8},{1,17},{2,10},{3,19},{4,12},{5,21},{6,14},{7,23},{8,0},{9,25... | collective-permute-start | bytes 12296 | tf_op jit(solution)/shard_map/ppermute | solution.py:44
  8.1 5.7 %collective-permute-start.5 = (f32[128,256]{1,0:T(8,128)S(1)}, f32[128,256]{1,0:T(8,128)S(1)}, u32[]{:S(2)}, u32[]{:S(2)}) collective-permute-start(f32[128,256]{1,0:T(8,128)S(1)} %pair.1.after.refs_0_), channel_id=1, source_target_pairs={{0,8},{1,17},{2,10},{3,19},{4,12},{5,21},{6,14},{7,23},{8,0},{9,25... | collective-permute-start | bytes 393224 | tf_op jit(solution)/shard_map/ppermute | solution.py:44
  9.4 5.8 %collective-permute-start.4 = (f32[128,256]{1,0:T(8,128)S(1)}, f32[128,256]{1,0:T(8,128)S(1)}, u32[]{:S(2)}, u32[]{:S(2)}) collective-permute-start(f32[128,256]{1,0:T(8,128)S(1)} %pair.1.after.refs_0_), channel_id=1, source_target_pairs={{0,2},{1,25},{2,0},{3,27},{4,6},{5,29},{6,4},{7,31},{8,10},{9,17},... | collective-permute-start | bytes 393224 | tf_op jit(solution)/shard_map/ppermute | solution.py:44
  11.3 9.5 %collective-permute-start.8 = (f32[8,128,128]{2,1,0:T(8,128)S(1)}, f32[8,128,128]{2,1,0:T(8,128)S(1)}, u32[]{:S(2)}, u32[]{:S(2)}) collective-permute-start(f32[8,128,128]{2,1,0:T(8,128)S(1)} %send.1.after), channel_id=1, source_target_pairs={{0,16},{1,9},{2,18},{3,11},{4,20},{5,13},{6,22},{7,15},{8,24},{9,1... | collective-permute-start | bytes 1572872 | tf_op jit(solution)/shard_map/ppermute | solution.py:44
  15.2 1.8 %collective-permute-start.7 = (f32[384,256]{1,0:T(8,128)S(1)}, f32[384,256]{1,0:T(8,128)S(1)}, u32[]{:S(2)}, u32[]{:S(2)}) collective-permute-start(f32[384,256]{1,0:T(8,128)S(1)} %merge.1.refs_1_), channel_id=1, source_target_pairs={{0,1},{1,0},{2,3},{3,2},{4,5},{5,4},{6,7},{7,6},{8,9},{9,8},{10,11... | collective-permute-start | bytes 1179656 | tf_op jit(solution)/shard_map/ppermute | solution.py:44

commit v5 on v3

--- a/solution.py
+++ b/solution.py
@@ -14,7 +14,7 @@
 LINES, LANES = 8, 128
 LOW, OWN, OUT, OTHER = 0, 1, 2, 3
 f32, i32 = jnp.float32, jnp.int32
-COST = dict(hint=1 << 33, label=0, pair=0, pack=0, send=1 << 30, mark=34 << 25, merge=0, part=0, last=0)
+COST = dict(hint=1 << 33, label=0, pair=0, pack=0, send=1 << 30, tiles=0, mark=34 << 25, merge=0, part=0, last=0)
 
 
 class Plan:
@@ -46,6 +46,9 @@
     def swap(self, shard, stage):
         return self.move(shard, (self.offset(0, stage), 0), (self.offset(1, stage), 0))
 
+    def cross(self, shard, stage):
+        return self.move(shard, (self.offset(0, stage), 1), (self.offset(1, stage), 1))
+
     def is_odd(self):
         return lax.rem(lax.axis_index("blk"), 2) == 1
 
@@ -67,18 +70,22 @@
     mark[...] = jnp.zeros_like(mark)
 
 
-def label_kernel(mark, low, own, out, maps):
+def label_kernel(n, mark, panel, low, own, out, maps, labelled):
     maps[...] = jnp.zeros_like(maps)
     for line, ref in ((LOW, low), (OWN, own), (OUT, out)):
         maps[line : line + 1, 0 : ref.shape[2]] = ref[0]
-
-
-def pair_kernel(n, after, own, other, joined):
+    labelled[0:n] = panel[...]
+    labelled[n:] = jnp.zeros((LINES, labelled.shape[1]), f32)
+    labelled[n:, 0:LANES] = maps[...].astype(f32)
+
+
+def pair_kernel(n, after, own, other, joined, maps):
     joined[0:n] = own[...]
-    joined[n : 2 * n] = other[...]
-
-
-def pack_kernel(after, own, other, maps):
+    joined[n : 2 * n] = other[0:n]
+    maps[...] = other[n:, 0:LANES].astype(i32)
+
+
+def pack_kernel(own, other, maps):
     maps[...] = jnp.zeros_like(maps)
     maps[0:OTHER] = own[0:OTHER]
     maps[OTHER : 2 * OTHER] = other[0:OTHER]
@@ -97,11 +104,11 @@
     return [values[0, u] for u in range(count)]
 
 
-def send_kernel(plan, maps, maps_met, mine, met, sent):
+def send_kernel(plan, turned, maps, maps_met, mine, met, sent):
     line = lambda ref, k: jnp.broadcast_to(ref[k : k + 1, :], (LINES, LANES))
     through = lambda targets, slots: jnp.take_along_axis(targets, slots, axis=1, mode="promise_in_bounds")
     if plan.balanced:
-        odd = plan.is_odd()
+        odd = plan.is_odd() == turned
         own_slots = jnp.where(odd, through(line(maps, OTHER + OWN), line(maps, LOW)), line(maps, OUT))
         target = jnp.where(odd, line(maps_met, OTHER + OUT), line(maps, OUT))
         met_slots = through(target, line(maps_met, LOW))
@@ -115,10 +122,9 @@
         sent[slot] += met[0, 0, u]
 
 
-def part_kernel(plan, places, maps, maps_met, mine, met, *refs):
-    part, tiles, left, right = refs[-4:]
-    n, size = plan.part_rows, plan.size
-    odd = plan.is_odd()
+def tiles_kernel(plan, turned, maps, maps_met, mine, met, *refs):
+    parts, tiles = refs[:-1], refs[-1]
+    odd = plan.is_odd() == turned
     tiles[...] = jnp.zeros_like(tiles)
     for u in range(plan.slots):
         tiles[maps[OWN, u]] += mine[0, 0, u]
@@ -127,6 +133,15 @@
         if plan.balanced:
             slot = jnp.where(odd, maps_met[OUT, u], slot)
         tiles[slot] += met[0, 0, u]
+    count = plan.tiles // len(parts)
+    for k, ref in enumerate(parts):
+        ref[...] = tiles[k * count : (k + 1) * count]
+
+
+def part_kernel(plan, places, upper, lower, *refs):
+    part, left, right = refs[-3:]
+    n, size = plan.part_rows, plan.size
+    odd = plan.is_odd()
 
     def lay(parity):
         for ref, chunks in zip(refs, places[parity]):
@@ -141,8 +156,7 @@
         pl.when(jnp.logical_not(odd))(functools.partial(lay, 0))
         pl.when(odd)(functools.partial(lay, 1))
 
-    @pl.loop(0, plan.rows // size)
-    def _(i):
+    def strip(i, tiles, k):
         panel = left[pl.ds(pl.multiple_of(i * size, size), size), :]
         for j in range(plan.across):
             product = lax.dot_general(
@@ -153,8 +167,12 @@
                 preferred_element_type=f32,
             )
             part[pl.ds(pl.multiple_of(i * size, size), size), j * size : (j + 1) * size] = (
-                tiles[i * plan.across + j] - product
+                tiles[k * plan.across + j] - product
             )
+
+    half = plan.rows // size // 2
+    pl.loop(0, half)(lambda i: strip(i, upper, i))
+    pl.loop(0, half)(lambda i: strip(half + i, lower, i))
 
 
 def last_kernel(plan, *refs):
@@ -176,28 +194,36 @@
     return lax.optimization_barrier((first, *then))[1:]
 
 
-def add_sent(plan, maps, updates, met):
+def add_sent(plan, turned, maps, updates, met):
     return call(
-        functools.partial(send_kernel, plan),
+        functools.partial(send_kernel, plan, turned),
         jax.ShapeDtypeStruct(updates.shape[2:], f32),
-        [VMEM] * (len(maps) + 2),
+        [VMEM] * 4,
         (*maps, updates, met),
         "send",
     )
 
 
-def add_part(plan, places, maps, updates, met, panels):
+def add_tiles(plan, turned, maps, updates, met):
+    return call(
+        functools.partial(tiles_kernel, plan, turned),
+        [jax.ShapeDtypeStruct((plan.tiles // 2, plan.size, plan.size), f32)] * 2,
+        [SMEM] * 2 + [VMEM] * 2,
+        (*maps, updates, met),
+        "tiles",
+        [pltpu.VMEM((plan.tiles, plan.size, plan.size), f32)],
+        limit=24,
+    )
+
+
+def add_part(plan, places, tiles, panels):
     return call(
         functools.partial(part_kernel, plan, places),
         jax.ShapeDtypeStruct((plan.rows, plan.cols), f32),
-        [SMEM] * 2 + [VMEM] * (2 + len(panels)),
-        (*maps, updates, met, *panels),
+        [VMEM] * (2 + len(panels)),
+        (*tiles, *panels),
         "part",
-        [
-            pltpu.VMEM((plan.tiles, plan.size, plan.size), f32),
-            pltpu.VMEM((plan.rows, plan.depth), f32),
-            pltpu.VMEM((plan.cols, plan.depth), f32),
-        ],
+        [pltpu.VMEM((plan.rows, plan.depth), f32), pltpu.VMEM((plan.cols, plan.depth), f32)],
         limit=40,
     )
 
@@ -220,7 +246,7 @@
     own_maps = jnp.pad(own_maps, ((0, 0), (0, LANES - plan.slots)))
     maps = jnp.concatenate([own_maps, plan.swap(own_maps, 1)])
     maps_met = plan.swap(maps, 0)
-    got = plan.swap(add_sent(plan, [maps, maps_met], updates, met), 1)
+    got = plan.swap(add_sent(plan, True, [maps, maps_met], updates, met), 1)
     panels, places = [pivot_panel], [[[(ROW, 0), (COL, 0)]]]
     for c in range(1, plan.cubes):
         panels.append(plan.move(pivot_panel, (c, 0), (c, 0)))
@@ -228,39 +254,48 @@
     for b in range(1, plan.blks):
         panels.append(plan.move(pivot_panel, (0, b), (0, b)))
         places.append([[(COL, b)]])
-    part = add_part(plan, (places, places), (maps, maps_met), updates, met, panels)
+    tiles = add_tiles(plan, True, (maps, maps_met), updates, met)
+    part = add_part(plan, (places, places), tiles, panels)
     return add_last(plan, [] if plan.balanced else [maps], part, got)
 
 
 def four_by_eight(plan, updates, pivot_panel, map_low, map_own, map_out):
     n, depth = plan.part_rows, plan.depth
+    x, y = plan.low, plan.up
     shape = jax.ShapeDtypeStruct
-    met = plan.swap(updates, 0)
+    sibling = lambda shard: plan.move(shard, (0, 1), (0, 1))
+    met = plan.cross(updates, 0)
     mark = call(hint_kernel, shape((LINES, LANES), f32), [], (), "hint")
-    (panel_late,) = after(mark, pivot_panel)
-    sibling = plan.move(panel_late, (0, 1), (0, 1))
     lines = shape((LINES, LANES), i32)
-    own_maps = call(label_kernel, lines, [VMEM] * 4, (mark, map_low, map_own, map_out), "label")
-    other_maps = plan.swap(own_maps, 1)
-    pair = call(
+    own_maps, labelled = call(
+        functools.partial(label_kernel, n),
+        [lines, shape((n + LINES, depth), f32)],
+        [VMEM] * 5,
+        (mark, pivot_panel, map_low, map_own, map_out),
+        "label",
+    )
+    other_maps = plan.cross(own_maps, 1)
+    twin = sibling(updates)
+    pair, twin_maps = call(
         functools.partial(pair_kernel, n),
-        shape((2 * n, depth), f32),
+        [shape((2 * n, depth), f32), lines],
         [VMEM] * 3,
-        (own_maps, pivot_panel, sibling),
+        (twin, pivot_panel, sibling(labelled)),
         "pair",
     )
     along = plan.move(pair, (0, 4), (0, 6))
-    maps = call(pack_kernel, lines, [VMEM] * 3, (pair, own_maps, other_maps), "pack")
-    maps_met = plan.swap(maps, 0)
+    maps = call(pack_kernel, lines, [VMEM] * 2, (twin_maps, other_maps), "pack")
+    maps_met = plan.move(maps, (y, 0), (x, 0))
     (pair_late,) = after(maps, pair)
-    x, y = plan.low, plan.up
     near = plan.move(pair_late, (x, 0), (y, 0))
     far = plan.move(pair_late, (x ^ y, 0), (0, 2))
 
-    sent = add_sent(plan, [maps, maps_met], updates, met)
-    got = plan.swap(sent, 1)
-
-    mark = call(mark_kernel, shape((LINES, LANES), f32), [VMEM] * 2, (sent, along), "mark")
+    sent = add_sent(plan, False, [maps, maps_met], twin, met)
+    got = plan.move(sent, (x, 1), (y, 1))
+    sent, twin_late, met_late = lax.optimization_barrier((sent, twin, met))
+    tiles = add_tiles(plan, False, (maps, maps_met), twin_late, met_late)
+
+    mark = call(mark_kernel, shape((LINES, LANES), f32), [VMEM] * 2, (tiles[0], along), "mark")
     far, near, mark = lax.optimization_barrier((far, near, mark))
     merged = call(
         functools.partial(merge_kernel, n),
@@ -269,13 +304,13 @@
         (mark, near, far, along),
         "merge",
     )
-    shared = plan.move(merged, (0, 1), (0, 1))
+    shared = sibling(merged)
     own = [[(ROW, 0), (COL, 0)], [(COL, 1)]]
     cols = lambda b: [[(COL, b)], [(COL, b ^ 1)]]
     even = [own, cols(4) + [[(ROW, x)], [], [(ROW, x ^ y)], []], cols(7) + [[], [(ROW, y)]] + cols(3)]
     odd = [own, cols(6) + [[(ROW, y)], []] + cols(2), cols(5) + [[], [(ROW, x)], [], [(ROW, x ^ y)]]]
     panels = [pair, merged, shared]
-    part = add_part(plan, (even, odd), (maps, maps_met), updates, met, panels)
+    part = add_part(plan, (even, odd), [sibling(t) for t in tiles], panels)
     return add_last(plan, [], part, got)
 
 

time: 22 us -> 21.4 us (0.973)
  waiting for transfers between devices: 6.18 us -> 5.19 us
  starting transfers between devices: 12.4 us -> 12.8 us
    ppermute x9 -> x12, waiting for transfers between devices: 6.18 us -> 5.19 us  [move(): return lax.ppermute(shard, AXES, pairs)]
    ppermute x9 -> x12, starting transfers between devices: 12.4 us -> 12.8 us  [move(): return lax.ppermute(shard, AXES, pairs)]
    pallas_call x9 -> x10, Pallas kernels: 3.23 us -> 3.11 us  [call(): pl.pallas_call(kernel, out_shape=outs, in_specs=in_specs, out_specs=[VMEM...]
  transfers between devices with their start and end apart: 9 -> 12, of which waited for: 5 -> 7; matrix products, arithmetic and copies ran while one was open for 0% -> 0% of each run, Pallas kernels for 9% -> 9%
where the time goes in v5:
time: 21.4 us; the launch traced here: 21.2 us
  starting transfers between devices  12.8 us (60%)
  waiting for transfers between devices  5.19 us (24%)
  Pallas kernels  3.11 us (15%)
    ppermute x12, starting transfers between devices, move(): return lax.ppermute(shard, AXES, pairs)  12.8 us
    ppermute x12, waiting for transfers between devices, move(): return lax.ppermute(shard, AXES, pairs)  5.19 us
    pallas_call x10, Pallas kernels, call(): pl.pallas_call(kernel, out_shape=outs, in_specs=in_specs, out_specs=[VMEM...  3.11 us
  transfers between devices with their start and end apart: 12, of which 7 were waited for; matrix products, arithmetic and copies ran while one was open for 0% of the time, Pallas kernels for 9%

profile of v5, /device:TPU:0, one launch (start us, length us, event | category | flops | bytes accessed | tf_op | source)
XLA Modules:
  0.0 21.2 jit_solution(17595705847242048020)
XLA Ops:
  0.0 0.0 copy-start
  0.0 0.0 copy-start.1
  0.0 0.0 copy-start.2
  0.0 0.0 copy-start.3
  0.0 0.5 %collective-permute-start = (f32[1,1,8,128,128]{4,3,2,1,0:T(8,128)}, f32[1,1,8,128,128]{4,3,2,1,0:T(8,128)S(1)}, u32[]{:S(2)}, u32[]{:S(2)}) collective-permute-start(f32[1,1,8,128,128]{4,3,2,1,0:T(8,128)} %param.5), channel_id=1, source_target_pairs={{0,1},{1,0},{2,3},{3,2},{4,5},{5,4},{6,7},{7,6},{8,9},{9,8},{10,11... | collective-permute-start | bytes 1572872 | tf_op jit(solution)/shard_map/ppermute | solution.py:44
  0.5 2.6 %collective-permute-start.4 = (f32[1,1,8,128,128]{4,3,2,1,0:T(8,128)}, f32[1,1,8,128,128]{4,3,2,1,0:T(8,128)S(1)}, u32[]{:S(2)}, u32[]{:S(2)}) collective-permute-start(f32[1,1,8,128,128]{4,3,2,1,0:T(8,128)} %param.5), channel_id=1, source_target_pairs={{0,9},{1,16},{2,11},{3,18},{4,13},{5,20},{6,15},{7,22},{8,1},{9,24... | collective-permute-start | bytes 1572872 | tf_op jit(solution)/shard_map/ppermute | solution.py:44
  3.1 0.0 copy-done
  3.1 0.0 copy-done.1
  3.1 0.0 copy-done.2
  3.2 0.0 copy-done.3
  3.2 0.2 collective-permute-start.1
  3.3 1.5 %collective-permute-start.2 = (s32[8,128]{1,0:T(8,128)S(1)}, s32[8,128]{1,0:T(8,128)S(1)}, u32[]{:S(2)}, u32[]{:S(2)}) collective-permute-start(s32[8,128]{1,0:T(8,128)S(1)} %get-tuple-element.19), channel_id=1, source_target_pairs={{0,17},{1,8},{2,19},{3,10},{4,21},{5,12},{6,23},{7,14},{8,25},{9,0... | collective-permute-start | bytes 12296 | tf_op jit(solution)/shard_map/ppermute | solution.py:44
  4.9 0.0 collective-permute-done.1.other
  4.9 0.0 collective-permute-done.after.mine
  4.9 2.7 %collective-permute-start.9 = (f32[128,256]{1,0:T(8,128)S(1)}, f32[128,256]{1,0:T(8,128)S(1)}, u32[]{:S(2)}, u32[]{:S(2)}) collective-permute-start(f32[128,256]{1,0:T(8,128)S(1)} %get-tuple-element.25.refs_0_), channel_id=1, source_target_pairs={{0,4},{1,7},{2,6},{3,5},{4,0},{5,3},{6,2},{7,1},{8,12},{9,15},{10,... | collective-permute-start | bytes 393224 | tf_op jit(solution)/shard_map/ppermute | solution.py:44
  7.6 0.0 collective-permute-done.2.other
  7.6 1.1 %collective-permute-start.3 = (s32[8,128]{1,0:T(8,128)S(1)}, s32[8,128]{1,0:T(8,128)S(1)}, u32[]{:S(2)}, u32[]{:S(2)}) collective-permute-start(s32[8,128]{1,0:T(8,128)S(1)} %pack.1.maps), channel_id=1, source_target_pairs={{0,16},{1,9},{2,18},{3,11},{4,20},{5,13},{6,22},{7,15},{8,24},{9,1... | collective-permute-start | bytes 12296 | tf_op jit(solution)/shard_map/ppermute | solution.py:44
  8.7 1.2 %collective-permute-start.7 = (f32[128,256]{1,0:T(8,128)S(1)}, f32[128,256]{1,0:T(8,128)S(1)}, u32[]{:S(2)}, u32[]{:S(2)}) collective-permute-start(f32[128,256]{1,0:T(8,128)S(1)} %get-tuple-element.25.refs_0_), channel_id=1, source_target_pairs={{0,24},{1,3},{2,26},{3,1},{4,28},{5,7},{6,30},{7,5},{8,16},{9,11},... | collective-permute-start | bytes 393224 | tf_op jit(solution)/shard_map/ppermute | solution.py:44
  9.9 1.2 %collective-permute-start.8 = (f32[128,256]{1,0:T(8,128)S(1)}, f32[128,256]{1,0:T(8,128)S(1)}, u32[]{:S(2)}, u32[]{:S(2)}) collective-permute-start(f32[128,256]{1,0:T(8,128)S(1)} %get-tuple-element.25.refs_0_), channel_id=1, source_target_pairs={{0,8},{1,17},{2,10},{3,19},{4,12},{5,21},{6,14},{7,23},{8,0},{9,25... | collective-permute-start | bytes 393224 | tf_op jit(solution)/shard_map/ppermute | solution.py:44
  11.1 0.0 collective-permute-done.4.met
  11.1 0.1 collective-permute-done.3.maps_met
  11.2 0.3 %send.1 = f32[8,128,128]{2,1,0:T(8,128)S(1)} custom-call(s32[8,128]{1,0:T(8,128)S(1)} %pack.1.maps, s32[8,128]{1,0:T(8,128)S(1)} %collective-permute-done.3.maps_met, f32[1,1,8,128,128]{4,3,2,1,0:T(8,128)S(1)} %collective-permute-done.after.mine, f32[1,1,8,128,128]{4,3,2,1,0:T(8,128)S(1)} %collective-permute-done.4.met), custom_call_target="tpu_custom_call" | custom-call | flops 1073741824 | tf_op jit(solution)/shard_map/send/pallas_call | solution.py:57
  11.5 1.2 %collective-permute-start.11 = (f32[8,128,128]{2,1,0:T(8,128)S(1)}, f32[8,128,128]{2,1,0:T(8,128)S(1)}, u32[]{:S(2)}, u32[]{:S(2)}) collective-permute-start(f32[8,128,128]{2,1,0:T(8,128)S(1)} %send.1), channel_id=1, source_target_pairs={{0,9},{1,16},{2,11},{3,18},{4,13},{5,20},{6,15},{7,22},{8,1},{9,24... | collective-permute-start | bytes 1572872 | tf_op jit(solution)/shard_map/ppermute | solution.py:44
  12.7 0.9 %tiles.1 = (f32[4,128,128]{2,1,0:T(8,128)S(1)}, f32[4,128,128]{2,1,0:T(8,128)S(1)}) custom-call(s32[8,128]{1,0:T(8,128)S(1)} %pack.1.maps, s32[8,128]{1,0:T(8,128)S(1)} %collective-permute-done.3.maps_met, f32[1,1,8,128,128]{4,3,2,1,0:T(8,128)S(1)} %collective-permute-done.after.mine, f32[1,1,8,128,128]{4,3,2,1,0:T(8,128)S(1)} %collective-permute-done.4.met), custom_call_target="tpu_custom_call" | custom-call | tf_op jit(solution)/shard_map/tiles/pallas_call | solution.py:57
  13.6 0.8 %collective-permute-done.9.along = f32[128,256]{1,0:T(8,128)S(1)} collective-permute-done((f32[128,256]{1,0:T(8,128)S(1)}, f32[128,256]{1,0:T(8,128)S(1)}, u32[]{:S(2)}, u32[]{:S(2)}) %collective-permute-start.9) | collective-permute-done | bytes 131104 | tf_op jit(solution)/shard_map/ppermute | solution.py:44
  14.4 0.3 %collective-permute-done.7.far = f32[128,256]{1,0:T(8,128)S(1)} collective-permute-done((f32[128,256]{1,0:T(8,128)S(1)}, f32[128,256]{1,0:T(8,128)S(1)}, u32[]{:S(2)}, u32[]{:S(2)}) %collective-permute-start.7) | collective-permute-done | bytes 131104 | tf_op jit(solution)/shard_map/ppermute | solution.py:44
  14.7 0.8 %collective-permute-done.8.near = f32[128,256]{1,0:T(8,128)S(1)} collective-permute-done((f32[128,256]{1,0:T(8,128)S(1)}, f32[128,256]{1,0:T(8,128)S(1)}, u32[]{:S(2)}, u32[]{:S(2)}) %collective-permute-start.8) | collective-permute-done | bytes 131104 | tf_op jit(solution)/shard_map/ppermute | solution.py:44
  15.5 0.1 collective-permute-start.10
  15.6 0.5 %collective-permute-start.5 = (f32[4,128,128]{2,1,0:T(8,128)S(1)}, f32[4,128,128]{2,1,0:T(8,128)S(1)}, u32[]{:S(2)}, u32[]{:S(2)}) collective-permute-start(f32[4,128,128]{2,1,0:T(8,128)S(1)} %get-tuple-element.22.after), channel_id=1, source_target_pairs={{0,1},{1,0},{2,3},{3,2},{4,5},{5,4},{6,7},{7,6},{8,9},{9,8},{10,11... | collective-permute-start | bytes 786440 | tf_op jit(solution)/shard_map/ppermute | solution.py:44
  16.1 0.1 collective-permute-start.6
  16.1 1.5 %collective-permute-done.5.upper = f32[4,128,128]{2,1,0:T(8,128)S(1)} collective-permute-done((f32[4,128,128]{2,1,0:T(8,128)S(1)}, f32[4,128,128]{2,1,0:T(8,128)S(1)}, u32[]{:S(2)}, u32[]{:S(2)}) %collective-permute-start.5) | collective-permute-done | bytes 262176 | tf_op jit(solution)/shard_map/ppermute | solution.py:44
  17.6 0.4 %collective-permute-done.6.lower = f32[4,128,128]{2,1,0:T(8,128)S(1)} collective-permute-done((f32[4,128,128]{2,1,0:T(8,128)S(1)}, f32[4,128,128]{2,1,0:T(8,128)S(1)}, u32[]{:S(2)}, u32[]{:S(2)}) %collective-permute-start.6) | collective-permute-done | bytes 262176 | tf_op jit(solution)/shard_map/ppermute | solution.py:44
  18.0 0.0 collective-permute-done.10.refs_2_
  18.0 1.0 %part.1.refs_0_ = f32[256,512]{1,0:T(8,128)S(1)} custom-call(f32[4,128,128]{2,1,0:T(8,128)S(1)} %collective-permute-done.5.upper, f32[4,128,128]{2,1,0:T(8,128)S(1)} %collective-permute-done.6.lower, f32[128,256]{1,0:T(8,128)S(1)} %get-tuple-element.25.refs_0_, f32[384,256]{1,0:T(8,128)S(1)} %merge.1.refs_1_, f32[384,256]{1,0:T(8,128)S(1)} %collective-permute-done.10.refs_2_), custom_call_target="tpu_custom_call" | custom-call | tf_op jit(solution)/shard_map/part/pallas_call | solution.py:57
  19.1 1.3 %collective-permute-done.11.refs_1_ = f32[8,128,128]{2,1,0:T(8,128)S(1)} collective-permute-done((f32[8,128,128]{2,1,0:T(8,128)S(1)}, f32[8,128,128]{2,1,0:T(8,128)S(1)}, u32[]{:S(2)}, u32[]{:S(2)}) %collective-permute-start.11) | collective-permute-done | bytes 524320 | tf_op jit(solution)/shard_map/ppermute | solution.py:44
  20.4 0.8 %last.1 = f32[256,512]{1,0:T(8,128)} custom-call(f32[256,512]{1,0:T(8,128)S(1)} %part.1.refs_0_, f32[8,128,128]{2,1,0:T(8,128)S(1)} %collective-permute-done.11.refs_1_), custom_call_target="tpu_custom_call" | custom-call | tf_op jit(solution)/shard_map/last/pallas_call | solution.py:57
  (6 shorter events, 0.1 us)
Async XLA Ops:
  0.0 3.1 %copy-start = (f32[64,256]{1,0:T(8,128)S(1)}, f32[64,256]{1,0:T(8,128)}, u32[]{:S(2)}) copy-start(f32[64,256]{1,0:T(8,128)} %own.3) | copy-start | bytes 196612
  0.0 3.1 %copy-start.1 = (s32[1,1,8]{2,1,0:T(1,128)S(1)}, s32[1,1,8]{2,1,0:T(1,128)}, u32[]{:S(2)}) copy-start(s32[1,1,8]{2,1,0:T(1,128)} %low.1) | copy-start | bytes 100
  0.0 3.1 %copy-start.2 = (s32[1,1,8]{2,1,0:T(1,128)S(1)}, s32[1,1,8]{2,1,0:T(1,128)}, u32[]{:S(2)}) copy-start(s32[1,1,8]{2,1,0:T(1,128)} %own.2) | copy-start | bytes 100
  0.0 3.1 %copy-start.3 = (s32[1,1,8]{2,1,0:T(1,128)S(1)}, s32[1,1,8]{2,1,0:T(1,128)}, u32[]{:S(2)}) copy-start(s32[1,1,8]{2,1,0:T(1,128)} %out.1) | copy-start | bytes 100
  0.0 4.9 %collective-permute-start = (f32[1,1,8,128,128]{4,3,2,1,0:T(8,128)}, f32[1,1,8,128,128]{4,3,2,1,0:T(8,128)S(1)}, u32[]{:S(2)}, u32[]{:S(2)}) collective-permute-start(f32[1,1,8,128,128]{4,3,2,1,0:T(8,128)} %param.5), channel_id=1, source_target_pairs={{0,1},{1,0},{2,3},{3,2},{4,5},{5,4},{6,7},{7,6},{8,9},{9,8},{10,11... | collective-permute-start | bytes 1572872 | tf_op jit(solution)/shard_map/ppermute | solution.py:44
  0.5 10.5 %collective-permute-start.4 = (f32[1,1,8,128,128]{4,3,2,1,0:T(8,128)}, f32[1,1,8,128,128]{4,3,2,1,0:T(8,128)S(1)}, u32[]{:S(2)}, u32[]{:S(2)}) collective-permute-start(f32[1,1,8,128,128]{4,3,2,1,0:T(8,128)} %param.5), channel_id=1, source_target_pairs={{0,9},{1,16},{2,11},{3,18},{4,13},{5,20},{6,15},{7,22},{8,1},{9,24... | collective-permute-start | bytes 1572872 | tf_op jit(solution)/shard_map/ppermute | solution.py:44
  3.2 1.7 %collective-permute-start.1 = (f32[72,256]{1,0:T(8,128)S(1)}, f32[72,256]{1,0:T(8,128)S(1)}, u32[]{:S(2)}, u32[]{:S(2)}) collective-permute-start(f32[72,256]{1,0:T(8,128)S(1)} %get-tuple-element.17), channel_id=1, source_target_pairs={{0,1},{1,0},{2,3},{3,2},{4,5},{5,4},{6,7},{7,6},{8,9},{9,8},{10,11... | collective-permute-start | bytes 221192 | tf_op jit(solution)/shard_map/ppermute | solution.py:44
  3.3 4.2 %collective-permute-start.2 = (s32[8,128]{1,0:T(8,128)S(1)}, s32[8,128]{1,0:T(8,128)S(1)}, u32[]{:S(2)}, u32[]{:S(2)}) collective-permute-start(s32[8,128]{1,0:T(8,128)S(1)} %get-tuple-element.19), channel_id=1, source_target_pairs={{0,17},{1,8},{2,19},{3,10},{4,21},{5,12},{6,23},{7,14},{8,25},{9,0... | collective-permute-start | bytes 12296 | tf_op jit(solution)/shard_map/ppermute | solution.py:44
  4.9 9.5 %collective-permute-start.9 = (f32[128,256]{1,0:T(8,128)S(1)}, f32[128,256]{1,0:T(8,128)S(1)}, u32[]{:S(2)}, u32[]{:S(2)}) collective-permute-start(f32[128,256]{1,0:T(8,128)S(1)} %get-tuple-element.25.refs_0_), channel_id=1, source_target_pairs={{0,4},{1,7},{2,6},{3,5},{4,0},{5,3},{6,2},{7,1},{8,12},{9,15},{10,... | collective-permute-start | bytes 393224 | tf_op jit(solution)/shard_map/ppermute | solution.py:44
  7.6 3.6 %collective-permute-start.3 = (s32[8,128]{1,0:T(8,128)S(1)}, s32[8,128]{1,0:T(8,128)S(1)}, u32[]{:S(2)}, u32[]{:S(2)}) collective-permute-start(s32[8,128]{1,0:T(8,128)S(1)} %pack.1.maps), channel_id=1, source_target_pairs={{0,16},{1,9},{2,18},{3,11},{4,20},{5,13},{6,22},{7,15},{8,24},{9,1... | collective-permute-start | bytes 12296 | tf_op jit(solution)/shard_map/ppermute | solution.py:44
  8.7 6.0 %collective-permute-start.7 = (f32[128,256]{1,0:T(8,128)S(1)}, f32[128,256]{1,0:T(8,128)S(1)}, u32[]{:S(2)}, u32[]{:S(2)}) collective-permute-start(f32[128,256]{1,0:T(8,128)S(1)} %get-tuple-element.25.refs_0_), channel_id=1, source_target_pairs={{0,24},{1,3},{2,26},{3,1},{4,28},{5,7},{6,30},{7,5},{8,16},{9,11},... | collective-permute-start | bytes 393224 | tf_op jit(solution)/shard_map/ppermute | solution.py:44
  9.9 5.6 %collective-permute-start.8 = (f32[128,256]{1,0:T(8,128)S(1)}, f32[128,256]{1,0:T(8,128)S(1)}, u32[]{:S(2)}, u32[]{:S(2)}) collective-permute-start(f32[128,256]{1,0:T(8,128)S(1)} %get-tuple-element.25.refs_0_), channel_id=1, source_target_pairs={{0,8},{1,17},{2,10},{3,19},{4,12},{5,21},{6,14},{7,23},{8,0},{9,25... | collective-permute-start | bytes 393224 | tf_op jit(solution)/shard_map/ppermute | solution.py:44
  11.5 8.9 %collective-permute-start.11 = (f32[8,128,128]{2,1,0:T(8,128)S(1)}, f32[8,128,128]{2,1,0:T(8,128)S(1)}, u32[]{:S(2)}, u32[]{:S(2)}) collective-permute-start(f32[8,128,128]{2,1,0:T(8,128)S(1)} %send.1), channel_id=1, source_target_pairs={{0,9},{1,16},{2,11},{3,18},{4,13},{5,20},{6,15},{7,22},{8,1},{9,24... | collective-permute-start | bytes 1572872 | tf_op jit(solution)/shard_map/ppermute | solution.py:44
  15.5 2.5 %collective-permute-start.10 = (f32[384,256]{1,0:T(8,128)S(1)}, f32[384,256]{1,0:T(8,128)S(1)}, u32[]{:S(2)}, u32[]{:S(2)}) collective-permute-start(f32[384,256]{1,0:T(8,128)S(1)} %merge.1.refs_1_), channel_id=1, source_target_pairs={{0,1},{1,0},{2,3},{3,2},{4,5},{5,4},{6,7},{7,6},{8,9},{9,8},{10,11... | collective-permute-start | bytes 1179656 | tf_op jit(solution)/shard_map/ppermute | solution.py:44
  15.6 2.1 %collective-permute-start.5 = (f32[4,128,128]{2,1,0:T(8,128)S(1)}, f32[4,128,128]{2,1,0:T(8,128)S(1)}, u32[]{:S(2)}, u32[]{:S(2)}) collective-permute-start(f32[4,128,128]{2,1,0:T(8,128)S(1)} %get-tuple-element.22.after), channel_id=1, source_target_pairs={{0,1},{1,0},{2,3},{3,2},{4,5},{5,4},{6,7},{7,6},{8,9},{9,8},{10,11... | collective-permute-start | bytes 786440 | tf_op jit(solution)/shard_map/ppermute | solution.py:44
  16.1 2.0 %collective-permute-start.6 = (f32[4,128,128]{2,1,0:T(8,128)S(1)}, f32[4,128,128]{2,1,0:T(8,128)S(1)}, u32[]{:S(2)}, u32[]{:S(2)}) collective-permute-start(f32[4,128,128]{2,1,0:T(8,128)S(1)} %get-tuple-element.23), channel_id=1, source_target_pairs={{0,1},{1,0},{2,3},{3,2},{4,5},{5,4},{6,7},{7,6},{8,9},{9,8},{10,11... | collective-permute-start | bytes 786440 | tf_op jit(solution)/shard_map/ppermute | solution.py:44

commit v6 on v5

--- a/solution.py
+++ b/solution.py
@@ -283,12 +283,12 @@
         (twin, pivot_panel, sibling(labelled)),
         "pair",
     )
-    along = plan.move(pair, (0, 4), (0, 6))
+    along = plan.move(pair, (0, 2), (0, 6))
     maps = call(pack_kernel, lines, [VMEM] * 2, (twin_maps, other_maps), "pack")
     maps_met = plan.move(maps, (y, 0), (x, 0))
     (pair_late,) = after(maps, pair)
-    near = plan.move(pair_late, (x, 0), (y, 0))
-    far = plan.move(pair_late, (x ^ y, 0), (0, 2))
+    near = plan.move(pair_late, (x, 0), (0, 4))
+    far = plan.move(pair_late, (x ^ y, 0), (y, 0))
 
     sent = add_sent(plan, False, [maps, maps_met], twin, met)
     got = plan.move(sent, (x, 1), (y, 1))
@@ -307,8 +307,8 @@
     shared = sibling(merged)
     own = [[(ROW, 0), (COL, 0)], [(COL, 1)]]
     cols = lambda b: [[(COL, b)], [(COL, b ^ 1)]]
-    even = [own, cols(4) + [[(ROW, x)], [], [(ROW, x ^ y)], []], cols(7) + [[], [(ROW, y)]] + cols(3)]
-    odd = [own, cols(6) + [[(ROW, y)], []] + cols(2), cols(5) + [[], [(ROW, x)], [], [(ROW, x ^ y)]]]
+    even = [own, cols(2) + [[(ROW, x)], [], [(ROW, x ^ y)], []], cols(7) + cols(5) + [[], [(ROW, y)]]]
+    odd = [own, cols(6) + cols(4) + [[(ROW, y)], []], cols(3) + [[], [(ROW, x)], [], [(ROW, x ^ y)]]]
     panels = [pair, merged, shared]
     part = add_part(plan, (even, odd), [sibling(t) for t in tiles], panels)
     return add_last(plan, [], part, got)

time: 21.4 us -> 21.2 us (level)
  waiting for transfers between devices: 5.19 us -> 4.1 us
  starting transfers between devices: 12.8 us -> 13.8 us
    ppermute x12, waiting for transfers between devices: 5.19 us -> 4.1 us  [move(): return lax.ppermute(shard, AXES, pairs)]
    ppermute x12, starting transfers between devices: 12.8 us -> 13.8 us  [move(): return lax.ppermute(shard, AXES, pairs)]
  transfers between devices with their start and end apart: 12 -> 12, of which waited for: 7 -> 6; matrix products, arithmetic and copies ran while one was open for 0% -> 0% of each run, Pallas kernels for 9% -> 9%
where the time goes in v6:
time: 21.2 us; the launch traced here: 21.1 us
  starting transfers between devices  13.8 us (65%)
  waiting for transfers between devices  4.1 us (19%)
  Pallas kernels  3.11 us (15%)
    ppermute x12, starting transfers between devices, move(): return lax.ppermute(shard, AXES, pairs)  13.8 us
    ppermute x12, waiting for transfers between devices, move(): return lax.ppermute(shard, AXES, pairs)  4.1 us
    pallas_call x10, Pallas kernels, call(): pl.pallas_call(kernel, out_shape=outs, in_specs=in_specs, out_specs=[VMEM...  3.11 us
  transfers between devices with their start and end apart: 12, of which 6 were waited for; matrix products, arithmetic and copies ran while one was open for 0% of the time, Pallas kernels for 9%

profile of v6, /device:TPU:0, one launch (start us, length us, event | category | flops | bytes accessed | tf_op | source)
XLA Modules:
  0.0 21.1 jit_solution(18402622172841205874)
XLA Ops:
  0.0 0.0 copy-start
  0.0 0.0 copy-start.1
  0.0 0.0 copy-start.2
  0.0 0.0 copy-start.3
  0.0 0.5 %collective-permute-start = (f32[1,1,8,128,128]{4,3,2,1,0:T(8,128)}, f32[1,1,8,128,128]{4,3,2,1,0:T(8,128)S(1)}, u32[]{:S(2)}, u32[]{:S(2)}) collective-permute-start(f32[1,1,8,128,128]{4,3,2,1,0:T(8,128)} %param.5), channel_id=1, source_target_pairs={{0,1},{1,0},{2,3},{3,2},{4,5},{5,4},{6,7},{7,6},{8,9},{9,8},{10,11... | collective-permute-start | bytes 1572872 | tf_op jit(solution)/shard_map/ppermute | solution.py:44
  0.5 2.6 %collective-permute-start.4 = (f32[1,1,8,128,128]{4,3,2,1,0:T(8,128)}, f32[1,1,8,128,128]{4,3,2,1,0:T(8,128)S(1)}, u32[]{:S(2)}, u32[]{:S(2)}) collective-permute-start(f32[1,1,8,128,128]{4,3,2,1,0:T(8,128)} %param.5), channel_id=1, source_target_pairs={{0,9},{1,16},{2,11},{3,18},{4,13},{5,20},{6,15},{7,22},{8,1},{9,24... | collective-permute-start | bytes 1572872 | tf_op jit(solution)/shard_map/ppermute | solution.py:44
  3.1 0.0 copy-done
  3.1 0.0 copy-done.1
  3.1 0.0 copy-done.2
  3.2 0.0 copy-done.3
  3.2 0.2 collective-permute-start.1
  3.3 1.5 %collective-permute-start.2 = (s32[8,128]{1,0:T(8,128)S(1)}, s32[8,128]{1,0:T(8,128)S(1)}, u32[]{:S(2)}, u32[]{:S(2)}) collective-permute-start(s32[8,128]{1,0:T(8,128)S(1)} %get-tuple-element.19), channel_id=1, source_target_pairs={{0,17},{1,8},{2,19},{3,10},{4,21},{5,12},{6,23},{7,14},{8,25},{9,0... | collective-permute-start | bytes 12296 | tf_op jit(solution)/shard_map/ppermute | solution.py:44
  4.9 0.0 collective-permute-done.1.other
  4.9 0.0 collective-permute-done.after.mine
  4.9 1.6 %collective-permute-start.9 = (f32[128,256]{1,0:T(8,128)S(1)}, f32[128,256]{1,0:T(8,128)S(1)}, u32[]{:S(2)}, u32[]{:S(2)}) collective-permute-start(f32[128,256]{1,0:T(8,128)S(1)} %get-tuple-element.25.refs_0_), channel_id=1, source_target_pairs={{0,2},{1,7},{2,0},{3,5},{4,6},{5,3},{6,4},{7,1},{8,10},{9,15},{10,... | collective-permute-start | bytes 393224 | tf_op jit(solution)/shard_map/ppermute | solution.py:44
  6.5 0.0 collective-permute-done.2.other
  6.6 1.3 %collective-permute-start.3 = (s32[8,128]{1,0:T(8,128)S(1)}, s32[8,128]{1,0:T(8,128)S(1)}, u32[]{:S(2)}, u32[]{:S(2)}) collective-permute-start(s32[8,128]{1,0:T(8,128)S(1)} %pack.1.maps), channel_id=1, source_target_pairs={{0,16},{1,9},{2,18},{3,11},{4,20},{5,13},{6,22},{7,15},{8,24},{9,1... | collective-permute-start | bytes 12296 | tf_op jit(solution)/shard_map/ppermute | solution.py:44
  7.9 1.5 %collective-permute-start.7 = (f32[128,256]{1,0:T(8,128)S(1)}, f32[128,256]{1,0:T(8,128)S(1)}, u32[]{:S(2)}, u32[]{:S(2)}) collective-permute-start(f32[128,256]{1,0:T(8,128)S(1)} %get-tuple-element.25.refs_0_), channel_id=1, source_target_pairs={{0,24},{1,17},{2,26},{3,19},{4,28},{5,21},{6,30},{7,23},{8,16},{9,... | collective-permute-start | bytes 393224 | tf_op jit(solution)/shard_map/ppermute | solution.py:44
  9.4 0.7 %collective-permute-start.8 = (f32[128,256]{1,0:T(8,128)S(1)}, f32[128,256]{1,0:T(8,128)S(1)}, u32[]{:S(2)}, u32[]{:S(2)}) collective-permute-start(f32[128,256]{1,0:T(8,128)S(1)} %get-tuple-element.25.refs_0_), channel_id=1, source_target_pairs={{0,8},{1,5},{2,10},{3,7},{4,12},{5,1},{6,14},{7,3},{8,0},{9,13},{1... | collective-permute-start | bytes 393224 | tf_op jit(solution)/shard_map/ppermute | solution.py:44
  10.0 0.3 %collective-permute-done.4.met = f32[1,1,8,128,128]{4,3,2,1,0:T(8,128)S(1)} collective-permute-done((f32[1,1,8,128,128]{4,3,2,1,0:T(8,128)}, f32[1,1,8,128,128]{4,3,2,1,0:T(8,128)S(1)}, u32[]{:S(2)}, u32[]{:S(2)}) %collective-permute-start.4) | collective-permute-done | bytes 524320 | tf_op jit(solution)/shard_map/ppermute | solution.py:44
  10.3 0.0 collective-permute-done.3.maps_met
  10.3 0.3 %send.1 = f32[8,128,128]{2,1,0:T(8,128)S(1)} custom-call(s32[8,128]{1,0:T(8,128)S(1)} %pack.1.maps, s32[8,128]{1,0:T(8,128)S(1)} %collective-permute-done.3.maps_met, f32[1,1,8,128,128]{4,3,2,1,0:T(8,128)S(1)} %collective-permute-done.after.mine, f32[1,1,8,128,128]{4,3,2,1,0:T(8,128)S(1)} %collective-permute-done.4.met), custom_call_target="tpu_custom_call" | custom-call | flops 1073741824 | tf_op jit(solution)/shard_map/send/pallas_call | solution.py:57
  10.6 1.8 %collective-permute-start.11 = (f32[8,128,128]{2,1,0:T(8,128)S(1)}, f32[8,128,128]{2,1,0:T(8,128)S(1)}, u32[]{:S(2)}, u32[]{:S(2)}) collective-permute-start(f32[8,128,128]{2,1,0:T(8,128)S(1)} %send.1), channel_id=1, source_target_pairs={{0,9},{1,16},{2,11},{3,18},{4,13},{5,20},{6,15},{7,22},{8,1},{9,24... | collective-permute-start | bytes 1572872 | tf_op jit(solution)/shard_map/ppermute | solution.py:44
  12.5 0.9 %tiles.1 = (f32[4,128,128]{2,1,0:T(8,128)S(1)}, f32[4,128,128]{2,1,0:T(8,128)S(1)}) custom-call(s32[8,128]{1,0:T(8,128)S(1)} %pack.1.maps, s32[8,128]{1,0:T(8,128)S(1)} %collective-permute-done.3.maps_met, f32[1,1,8,128,128]{4,3,2,1,0:T(8,128)S(1)} %collective-permute-done.after.mine, f32[1,1,8,128,128]{4,3,2,1,0:T(8,128)S(1)} %collective-permute-done.4.met), custom_call_target="tpu_custom_call" | custom-call | tf_op jit(solution)/shard_map/tiles/pallas_call | solution.py:57
  13.3 0.0 collective-permute-done.9.along
  13.3 0.5 %collective-permute-done.7.far = f32[128,256]{1,0:T(8,128)S(1)} collective-permute-done((f32[128,256]{1,0:T(8,128)S(1)}, f32[128,256]{1,0:T(8,128)S(1)}, u32[]{:S(2)}, u32[]{:S(2)}) %collective-permute-start.7) | collective-permute-done | bytes 131104 | tf_op jit(solution)/shard_map/ppermute | solution.py:44
  13.9 0.6 %collective-permute-done.8.near = f32[128,256]{1,0:T(8,128)S(1)} collective-permute-done((f32[128,256]{1,0:T(8,128)S(1)}, f32[128,256]{1,0:T(8,128)S(1)}, u32[]{:S(2)}, u32[]{:S(2)}) %collective-permute-start.8) | collective-permute-done | bytes 131104 | tf_op jit(solution)/shard_map/ppermute | solution.py:44
  14.5 1.5 %collective-permute-start.10 = (f32[384,256]{1,0:T(8,128)S(1)}, f32[384,256]{1,0:T(8,128)S(1)}, u32[]{:S(2)}, u32[]{:S(2)}) collective-permute-start(f32[384,256]{1,0:T(8,128)S(1)} %merge.1.refs_1_), channel_id=1, source_target_pairs={{0,1},{1,0},{2,3},{3,2},{4,5},{5,4},{6,7},{7,6},{8,9},{9,8},{10,11... | collective-permute-start | bytes 1179656 | tf_op jit(solution)/shard_map/ppermute | solution.py:44
  16.0 0.1 collective-permute-start.5
  16.1 0.4 %collective-permute-start.6 = (f32[4,128,128]{2,1,0:T(8,128)S(1)}, f32[4,128,128]{2,1,0:T(8,128)S(1)}, u32[]{:S(2)}, u32[]{:S(2)}) collective-permute-start(f32[4,128,128]{2,1,0:T(8,128)S(1)} %get-tuple-element.23), channel_id=1, source_target_pairs={{0,1},{1,0},{2,3},{3,2},{4,5},{5,4},{6,7},{7,6},{8,9},{9,8},{10,11... | collective-permute-start | bytes 786440 | tf_op jit(solution)/shard_map/ppermute | solution.py:44
  16.5 1.2 %collective-permute-done.5.upper = f32[4,128,128]{2,1,0:T(8,128)S(1)} collective-permute-done((f32[4,128,128]{2,1,0:T(8,128)S(1)}, f32[4,128,128]{2,1,0:T(8,128)S(1)}, u32[]{:S(2)}, u32[]{:S(2)}) %collective-permute-start.5) | collective-permute-done | bytes 262176 | tf_op jit(solution)/shard_map/ppermute | solution.py:44
  17.7 0.4 %collective-permute-done.6.lower = f32[4,128,128]{2,1,0:T(8,128)S(1)} collective-permute-done((f32[4,128,128]{2,1,0:T(8,128)S(1)}, f32[4,128,128]{2,1,0:T(8,128)S(1)}, u32[]{:S(2)}, u32[]{:S(2)}) %collective-permute-start.6) | collective-permute-done | bytes 262176 | tf_op jit(solution)/shard_map/ppermute | solution.py:44
  18.1 0.0 collective-permute-done.10.refs_2_
  18.1 1.0 %part.1.refs_0_ = f32[256,512]{1,0:T(8,128)S(1)} custom-call(f32[4,128,128]{2,1,0:T(8,128)S(1)} %collective-permute-done.5.upper, f32[4,128,128]{2,1,0:T(8,128)S(1)} %collective-permute-done.6.lower, f32[128,256]{1,0:T(8,128)S(1)} %get-tuple-element.25.refs_0_, f32[384,256]{1,0:T(8,128)S(1)} %merge.1.refs_1_, f32[384,256]{1,0:T(8,128)S(1)} %collective-permute-done.10.refs_2_), custom_call_target="tpu_custom_call" | custom-call | tf_op jit(solution)/shard_map/part/pallas_call | solution.py:57
  19.1 1.1 %collective-permute-done.11.refs_1_ = f32[8,128,128]{2,1,0:T(8,128)S(1)} collective-permute-done((f32[8,128,128]{2,1,0:T(8,128)S(1)}, f32[8,128,128]{2,1,0:T(8,128)S(1)}, u32[]{:S(2)}, u32[]{:S(2)}) %collective-permute-start.11) | collective-permute-done | bytes 524320 | tf_op jit(solution)/shard_map/ppermute | solution.py:44
  20.3 0.8 %last.1 = f32[256,512]{1,0:T(8,128)} custom-call(f32[256,512]{1,0:T(8,128)S(1)} %part.1.refs_0_, f32[8,128,128]{2,1,0:T(8,128)S(1)} %collective-permute-done.11.refs_1_), custom_call_target="tpu_custom_call" | custom-call | tf_op jit(solution)/shard_map/last/pallas_call | solution.py:57
  (6 shorter events, 0.1 us)
Async XLA Ops:
  0.0 3.1 %copy-start = (f32[64,256]{1,0:T(8,128)S(1)}, f32[64,256]{1,0:T(8,128)}, u32[]{:S(2)}) copy-start(f32[64,256]{1,0:T(8,128)} %own.3) | copy-start | bytes 196612
  0.0 3.1 %copy-start.1 = (s32[1,1,8]{2,1,0:T(1,128)S(1)}, s32[1,1,8]{2,1,0:T(1,128)}, u32[]{:S(2)}) copy-start(s32[1,1,8]{2,1,0:T(1,128)} %low.1) | copy-start | bytes 100
  0.0 3.1 %copy-start.2 = (s32[1,1,8]{2,1,0:T(1,128)S(1)}, s32[1,1,8]{2,1,0:T(1,128)}, u32[]{:S(2)}) copy-start(s32[1,1,8]{2,1,0:T(1,128)} %own.2) | copy-start | bytes 100
  0.0 3.1 %copy-start.3 = (s32[1,1,8]{2,1,0:T(1,128)S(1)}, s32[1,1,8]{2,1,0:T(1,128)}, u32[]{:S(2)}) copy-start(s32[1,1,8]{2,1,0:T(1,128)} %out.1) | copy-start | bytes 100
  0.0 4.9 %collective-permute-start = (f32[1,1,8,128,128]{4,3,2,1,0:T(8,128)}, f32[1,1,8,128,128]{4,3,2,1,0:T(8,128)S(1)}, u32[]{:S(2)}, u32[]{:S(2)}) collective-permute-start(f32[1,1,8,128,128]{4,3,2,1,0:T(8,128)} %param.5), channel_id=1, source_target_pairs={{0,1},{1,0},{2,3},{3,2},{4,5},{5,4},{6,7},{7,6},{8,9},{9,8},{10,11... | collective-permute-start | bytes 1572872 | tf_op jit(solution)/shard_map/ppermute | solution.py:44
  0.5 9.8 %collective-permute-start.4 = (f32[1,1,8,128,128]{4,3,2,1,0:T(8,128)}, f32[1,1,8,128,128]{4,3,2,1,0:T(8,128)S(1)}, u32[]{:S(2)}, u32[]{:S(2)}) collective-permute-start(f32[1,1,8,128,128]{4,3,2,1,0:T(8,128)} %param.5), channel_id=1, source_target_pairs={{0,9},{1,16},{2,11},{3,18},{4,13},{5,20},{6,15},{7,22},{8,1},{9,24... | collective-permute-start | bytes 1572872 | tf_op jit(solution)/shard_map/ppermute | solution.py:44
  3.2 1.7 %collective-permute-start.1 = (f32[72,256]{1,0:T(8,128)S(1)}, f32[72,256]{1,0:T(8,128)S(1)}, u32[]{:S(2)}, u32[]{:S(2)}) collective-permute-start(f32[72,256]{1,0:T(8,128)S(1)} %get-tuple-element.17), channel_id=1, source_target_pairs={{0,1},{1,0},{2,3},{3,2},{4,5},{5,4},{6,7},{7,6},{8,9},{9,8},{10,11... | collective-permute-start | bytes 221192 | tf_op jit(solution)/shard_map/ppermute | solution.py:44
  3.3 3.2 %collective-permute-start.2 = (s32[8,128]{1,0:T(8,128)S(1)}, s32[8,128]{1,0:T(8,128)S(1)}, u32[]{:S(2)}, u32[]{:S(2)}) collective-permute-start(s32[8,128]{1,0:T(8,128)S(1)} %get-tuple-element.19), channel_id=1, source_target_pairs={{0,17},{1,8},{2,19},{3,10},{4,21},{5,12},{6,23},{7,14},{8,25},{9,0... | collective-permute-start | bytes 12296 | tf_op jit(solution)/shard_map/ppermute | solution.py:44
  4.9 8.4 %collective-permute-start.9 = (f32[128,256]{1,0:T(8,128)S(1)}, f32[128,256]{1,0:T(8,128)S(1)}, u32[]{:S(2)}, u32[]{:S(2)}) collective-permute-start(f32[128,256]{1,0:T(8,128)S(1)} %get-tuple-element.25.refs_0_), channel_id=1, source_target_pairs={{0,2},{1,7},{2,0},{3,5},{4,6},{5,3},{6,4},{7,1},{8,10},{9,15},{10,... | collective-permute-start | bytes 393224 | tf_op jit(solution)/shard_map/ppermute | solution.py:44
  6.6 3.8 %collective-permute-start.3 = (s32[8,128]{1,0:T(8,128)S(1)}, s32[8,128]{1,0:T(8,128)S(1)}, u32[]{:S(2)}, u32[]{:S(2)}) collective-permute-start(s32[8,128]{1,0:T(8,128)S(1)} %pack.1.maps), channel_id=1, source_target_pairs={{0,16},{1,9},{2,18},{3,11},{4,20},{5,13},{6,22},{7,15},{8,24},{9,1... | collective-permute-start | bytes 12296 | tf_op jit(solution)/shard_map/ppermute | solution.py:44
  7.9 6.0 %collective-permute-start.7 = (f32[128,256]{1,0:T(8,128)S(1)}, f32[128,256]{1,0:T(8,128)S(1)}, u32[]{:S(2)}, u32[]{:S(2)}) collective-permute-start(f32[128,256]{1,0:T(8,128)S(1)} %get-tuple-element.25.refs_0_), channel_id=1, source_target_pairs={{0,24},{1,17},{2,26},{3,19},{4,28},{5,21},{6,30},{7,23},{8,16},{9,... | collective-permute-start | bytes 393224 | tf_op jit(solution)/shard_map/ppermute | solution.py:44
  9.4 5.1 %collective-permute-start.8 = (f32[128,256]{1,0:T(8,128)S(1)}, f32[128,256]{1,0:T(8,128)S(1)}, u32[]{:S(2)}, u32[]{:S(2)}) collective-permute-start(f32[128,256]{1,0:T(8,128)S(1)} %get-tuple-element.25.refs_0_), channel_id=1, source_target_pairs={{0,8},{1,5},{2,10},{3,7},{4,12},{5,1},{6,14},{7,3},{8,0},{9,13},{1... | collective-permute-start | bytes 393224 | tf_op jit(solution)/shard_map/ppermute | solution.py:44
  10.6 9.6 %collective-permute-start.11 = (f32[8,128,128]{2,1,0:T(8,128)S(1)}, f32[8,128,128]{2,1,0:T(8,128)S(1)}, u32[]{:S(2)}, u32[]{:S(2)}) collective-permute-start(f32[8,128,128]{2,1,0:T(8,128)S(1)} %send.1), channel_id=1, source_target_pairs={{0,9},{1,16},{2,11},{3,18},{4,13},{5,20},{6,15},{7,22},{8,1},{9,24... | collective-permute-start | bytes 1572872 | tf_op jit(solution)/shard_map/ppermute | solution.py:44
  14.5 3.6 %collective-permute-start.10 = (f32[384,256]{1,0:T(8,128)S(1)}, f32[384,256]{1,0:T(8,128)S(1)}, u32[]{:S(2)}, u32[]{:S(2)}) collective-permute-start(f32[384,256]{1,0:T(8,128)S(1)} %merge.1.refs_1_), channel_id=1, source_target_pairs={{0,1},{1,0},{2,3},{3,2},{4,5},{5,4},{6,7},{7,6},{8,9},{9,8},{10,11... | collective-permute-start | bytes 1179656 | tf_op jit(solution)/shard_map/ppermute | solution.py:44
  16.0 1.7 %collective-permute-start.5 = (f32[4,128,128]{2,1,0:T(8,128)S(1)}, f32[4,128,128]{2,1,0:T(8,128)S(1)}, u32[]{:S(2)}, u32[]{:S(2)}) collective-permute-start(f32[4,128,128]{2,1,0:T(8,128)S(1)} %get-tuple-element.22.after), channel_id=1, source_target_pairs={{0,1},{1,0},{2,3},{3,2},{4,5},{5,4},{6,7},{7,6},{8,9},{9,8},{10,11... | collective-permute-start | bytes 786440 | tf_op jit(solution)/shard_map/ppermute | solution.py:44
  16.1 2.0 %collective-permute-start.6 = (f32[4,128,128]{2,1,0:T(8,128)S(1)}, f32[4,128,128]{2,1,0:T(8,128)S(1)}, u32[]{:S(2)}, u32[]{:S(2)}) collective-permute-start(f32[4,128,128]{2,1,0:T(8,128)S(1)} %get-tuple-element.23), channel_id=1, source_target_pairs={{0,1},{1,0},{2,3},{3,2},{4,5},{5,4},{6,7},{7,6},{8,9},{9,8},{10,11... | collective-permute-start | bytes 786440 | tf_op jit(solution)/shard_map/ppermute | solution.py:44
